TPU v7x, 32 devices: a whole 2x2x4 slice. The times are simulated.
32 devices in a mesh: mesh: 16 (over z, x, core), modes: 2 (over y).
Axes of the slice: x: 2, y: 2, z: 4, core: 2. Of those that a mesh axis runs over, the one named last changes fastest.
Arguments:
- subspace: float32 [64, 3, 16, 9216], P('modes', None, 'mesh'), may hold values from -14 to 14
- classes: int32 [16, 9216], P('mesh'), may hold values from 0 to 15
- level_density: float32 [16], replicated, may hold values from 0.05 to 1
Outputs:
- residual: float32 [64, 3, 16, 9216], P('modes', None, 'mesh')
- ritz_matrix: float32 [64, 64], replicated
All inputs are finite; a program needn't handle non-finite values.
Results may differ from a plain program's by a relative error of at most 0.0003.
Values sent between devices are 32-bit elements; how exact they have to be, the bound alone decides.
A program may use at most 128 MiB of HBM per device.

v0:
```python
import jax
import jax.numpy as jnp
import numpy as np
from jax import lax
from jax.sharding import PartitionSpec as P

NX = 96
NY = 96


highest = lax.Precision.HIGHEST
floor_modulus = 0.001


def shifted(x, axis, by):
    size = lax.axis_size(axis)
    pairs = [(i, i + by) for i in range(size) if 0 <= i + by < size]
    return lax.ppermute(x, axis, pairs)


def element_matrix():
    poisson_ratio = 0.3
    lame_first = poisson_ratio / ((1 + poisson_ratio) * (1 - 2 * poisson_ratio))
    shear_modulus = 1.0 / (2 * (1 + poisson_ratio))
    elastic = np.zeros((6, 6))
    elastic[:3, :3] = lame_first
    for normal_index in range(3):
        elastic[normal_index, normal_index] = lame_first + 2 * shear_modulus
        elastic[normal_index + 3, normal_index + 3] = shear_modulus
    corner_signs = [
        (1 - 2 * (corner & 1), 1 - 2 * (corner >> 1 & 1), 1 - 2 * (corner >> 2))
        for corner in range(8)
    ]
    gauss_point = 1.0 / np.sqrt(3.0)
    matrix = np.zeros((24, 24))
    for gauss_x in (-gauss_point, gauss_point):
        for gauss_y in (-gauss_point, gauss_point):
            for gauss_z in (-gauss_point, gauss_point):
                strain = np.zeros((6, 24))
                for corner in range(8):
                    sign_x, sign_y, sign_z = corner_signs[corner]
                    deriv_x = 2 * sign_x * (1 + sign_y * gauss_y) * (1 + sign_z * gauss_z) / 8
                    deriv_y = 2 * sign_y * (1 + sign_x * gauss_x) * (1 + sign_z * gauss_z) / 8
                    deriv_z = 2 * sign_z * (1 + sign_x * gauss_x) * (1 + sign_y * gauss_y) / 8
                    column = 3 * corner
                    strain[0, column] = deriv_x
                    strain[1, column + 1] = deriv_y
                    strain[2, column + 2] = deriv_z
                    strain[3, column] = deriv_y
                    strain[3, column + 1] = deriv_x
                    strain[4, column + 1] = deriv_z
                    strain[4, column + 2] = deriv_y
                    strain[5, column] = deriv_z
                    strain[5, column + 2] = deriv_x
                matrix = matrix + strain.T @ elastic @ strain / 8
    return matrix.reshape(8, 3, 8, 3)


def shift_in(plane, step_x, step_y, width_x):
    offset = step_x + step_y * width_x
    moved = plane
    if offset > 0:
        moved = jnp.pad(plane[..., :-offset], [(0, 0)] * (plane.ndim - 1) + [(offset, 0)])
    if step_x:
        column = lax.iota(jnp.int32, plane.shape[-1]) % width_x
        moved = jnp.where(column >= 1, moved, 0.0)
    return moved


def shift_out(force, step_x, step_y, width_x):
    moved = force
    if step_x:
        column = lax.iota(jnp.int32, force.shape[-1]) % width_x
        moved = jnp.where(column >= 1, moved, 0.0)
    offset = step_x + step_y * width_x
    if offset > 0:
        moved = jnp.pad(moved[..., offset:], [(0, 0)] * (force.ndim - 1) + [(0, offset)])
    return moved


def layer_forces(bottom, top, modulus_row, element, width_x):
    corners = []
    for step_z in (0, 1):
        source = top if step_z == 0 else bottom
        for step_y in (0, 1):
            for step_x in (0, 1):
                corners.append(shift_in(source, step_x, step_y, width_x))
    stacked = jnp.stack(corners, 0)
    forces = jnp.einsum("acbd,bkdn->akcn", element, stacked, precision=highest) * modulus_row
    force_top = jnp.zeros_like(top)
    force_bottom = jnp.zeros_like(bottom)
    for corner in range(8):
        moved_force = shift_out(forces[corner], corner & 1, corner >> 1 & 1, width_x)
        if corner >> 2 == 0:
            force_top = force_top + moved_force
        else:
            force_bottom = force_bottom + moved_force
    return (force_bottom, force_top)


def layer_sweep(vectors, below, modulus, element):
    plane_count = vectors.shape[2]
    totals = [jnp.zeros_like(below) for unused in range(plane_count + 1)]
    force_bottom, force_top = layer_forces(below, vectors[:, :, 0], modulus[0], element, NX)
    totals[0] = force_bottom
    totals[1] = force_top
    return (totals[0], jnp.stack(totals[1:], 2))


def apply_first(vectors, modulus, element):
    below = shifted(vectors[:, :, -1], "mesh", 1)
    force_bottom, stiff_image = layer_sweep(vectors, below, modulus, element)
    received = shifted(force_bottom, "mesh", -1)
    return stiff_image.at[:, :, -1].add(received)


def apply_again(vectors, modulus, element):
    below = shifted(vectors[:, :, -1], "mesh", 1)
    force_bottom, stiff_image = layer_sweep(vectors, below, modulus, element)
    received = shifted(force_bottom, "mesh", -1)
    return stiff_image.at[:, :, -1].add(received)


def densities(classes, level_density):
    levels = level_density.shape[0]
    level_index = lax.iota(jnp.int32, levels).reshape(levels, 1, 1)
    matches = classes[None] == level_index
    return jnp.sum(jnp.where(matches, level_density[:, None, None], 0.0), 0)


def ritz_solve(gram_stiff, gram_mass):
    lower_factor = jnp.linalg.cholesky(gram_mass)
    identity = jnp.eye(gram_mass.shape[0], dtype=jnp.float32)
    inverse = jax.scipy.linalg.solve_triangular(lower_factor, identity, lower=True)
    rotate = inverse.T
    ritz_matrix = jnp.dot(
        jnp.dot(inverse, gram_stiff, precision=highest, preferred_element_type=jnp.float32),
        rotate,
        precision=highest,
        preferred_element_type=jnp.float32,
    )
    mixed_rotate = jnp.dot(
        rotate, ritz_matrix, precision=highest, preferred_element_type=jnp.float32
    )
    return (ritz_matrix, rotate, mixed_rotate)


def per_device(subspace, classes, level_density):
    mode_count = subspace.shape[0]
    total_dofs = 3 * NX * NY * subspace.shape[2] * lax.axis_size("mesh")
    own_start = lax.axis_index("modes") * mode_count
    element = jnp.asarray(element_matrix(), jnp.float32)
    density = densities(classes, level_density)
    modulus = floor_modulus + (1.0 - floor_modulus) * density * density * density
    stiff_image = apply_first(subspace, modulus, element)
    mass_basis = subspace * density[None, None]
    all_modes = lax.all_gather(subspace, "modes", axis=0, tiled=True)
    tile_stiff = jnp.einsum("kczn,jczn->kj", all_modes, stiff_image, precision=highest)
    tile_mass = jnp.einsum("kczn,jczn->kj", all_modes, mass_basis, precision=highest)
    summed_stiff, summed_mass = lax.psum((tile_stiff, tile_mass), "mesh")
    gram_stiff, gram_mass = (
        lax.all_gather(summed_stiff, "modes", axis=1, tiled=True),
        lax.all_gather(summed_mass, "modes", axis=1, tiled=True),
    )
    gram_stiff = gram_stiff / total_dofs
    gram_mass = gram_mass / total_dofs
    ritz_matrix, rotate, mixed_rotate = ritz_solve(gram_stiff, gram_mass)
    own_rotate = lax.dynamic_slice_in_dim(rotate, own_start, mode_count, 1)
    own_mixed = lax.dynamic_slice_in_dim(mixed_rotate, own_start, mode_count, 1)
    rotated = jnp.einsum("kczn,kj->jczn", all_modes, own_rotate, precision=highest)
    rotated_mixed = jnp.einsum("kczn,kj->jczn", all_modes, own_mixed, precision=highest)
    residual = apply_again(rotated, modulus, element) - density[None, None] * rotated_mixed
    return (residual, ritz_matrix)


def solution(mesh):
    in_specs = (P("modes", None, "mesh", None), P("mesh", None), P())
    out_specs = (P("modes", None, "mesh", None), P())
    return jax.shard_map(
        per_device, mesh=mesh, in_specs=in_specs, out_specs=out_specs, check_vma=False
    )
```

profile of v0, /device:TPU:1, one launch (start us, length us, event | category | flops | bytes accessed | tf_op | source)
XLA Modules:
  0.0 527.9 jit_solution(12721036927791825883)
XLA Ops:
  7.2 4.4 copy.67
  11.6 2.0 copy-done.1
  13.6 4.6 collective-permute-start.2
  18.3 2.7 bitcast_dynamic-update-slice_fusion.7
  22.6 1.0 bitcast_dynamic-update-slice_fusion.6
  23.6 1.0 bitcast_dynamic-update-slice_fusion.5
  24.6 1.0 bitcast_dynamic-update-slice_fusion.4
  25.5 31.1 %collective-permute-done.2 = f32[32,3,9216]{2,0,1:T(8,128)S(1)} collective-permute-done((f32[32,3,9216]{2,0,1:T(8,128)S(1)}, f32[32,3,9216]{2,0,1:T(8,128)S(1)}, u32[]{:S(2)}, u32[]{:S(2)}) %collective-permute-start.2) | collective-permute-done | bytes 3538976 | tf_op jit(solution)/shard_map/ppermute | solution.py:18
  56.9 1.0 bitcast_dynamic-update-slice_fusion.2
  58.9 1.0 bitcast_dynamic-update-slice_fusion
  59.9 9.3 %copy-done.3 = f32[8,32,3,9216]{3,1,2,0:T(8,128)} copy-done((f32[8,32,3,9216]{3,1,2,0:T(8,128)}, f32[8,32,3,9216]{3,1,2,0:T(8,128)S(1)}, u32[]{:S(2)}) %copy-start.3) | copy-done | bytes 28311576
  69.2 58.1 %fusion.9 = f32[32,9216,8,3]{1,2,3,0:T(8,128)S(1)} fusion(f32[8,3,8,3,1]{2,0,3,1,4:T(8,128)S(1)} %copy-done.13, f32[8,32,3,9216,1]{3,1,2,0,4:T(8,128)} %bitcast.200), kind=kOutput, calls=%fused_computation.9 | convolution fusion | flops 2038431744 | bytes 56625408 | tf_op jit(solution)/shard_map/acbd,bkdn->akcn/dot_general | solution.py:89
  127.4 18.7 %fusion.4 = f32[8,32,3,9216]{3,1,2,0:T(8,128)} fusion(f32[32,9216,8,3]{1,2,3,0:T(8,128)S(1)} %fusion.9, f32[9216]{0:T(1024)S(1)} %fusion.54), kind=kLoop, calls=%fused_computation.5 | loop fusion | flops 7077888 | bytes 56659968 | tf_op jit(solution)/shard_map/mul | solution.py:89
  146.1 11.3 %slice_bitcast_fusion.6 = (f32[32,3,9216]{2,0,1:T(8,128)S(1)}, f32[32,3,9216]{2,0,1:T(8,128)S(1)}, f32[32,3,9216]{2,0,1:T(8,128)S(1)}, f32[32,3,9216]{2,0,1:T(8,...) fusion(f32[8,32,3,9216]{3,1,2,0:T(8,128)} %fusion.4), kind=kLoop, calls=%fused_computation.31 | loop fusion | bytes 42467328 | tf_op jit(solution)/shard_map/squeeze | solution.py:93
  158.3 1.0 copy-done.8
  159.3 3.6 slice_select_fusion.2
  162.9 3.6 slice_select_fusion.3
  166.6 4.6 fusion.21
  171.2 1.9 collective-permute-start.3
  173.2 4.9 slice.255
  178.0 8.6 %fusion.43 = f32[64,32]{0,1:T(8,128)} fusion(f32[64,3,1,9216]{3,0,1,2:T(8,128)} %all-gather.2.cloned.1.call-done, f32[32,3,1,9216]{3,2,1,0:T(1,128)S(1)} %copy-done.4, f32[9216]{0:T(1024)} %copy-done.9), kind=kOutput, calls=%fused_computation.80 | convolution fusion | flops 680361984 | bytes 10661888 | tf_op jit(solution)/shard_map/kczn,jczn->kj/dot_general | solution.py:159
  186.7 28.4 %collective-permute-done.3 = f32[32,3,9216]{2,0,1:T(8,128)} collective-permute-done((f32[32,3,9216]{2,0,1:T(8,128)}, f32[32,3,9216]{2,0,1:T(8,128)}, u32[]{:S(2)}, u32[]{:S(2)}) %collective-permute-start.3) | collective-permute-done | bytes 3538976 | tf_op jit(solution)/shard_map/ppermute | solution.py:18
  215.1 9.3 %fusion.48 = f32[64,32]{0,1:T(8,128)S(1)} fusion(f32[64,3,1,9216]{3,0,1,2:T(8,128)S(1)} %copy-done, f32[32,3,9216]{2,0,1:T(8,128)} %collective-permute-done.3, f32[8,32,3,9216]{3,1,2,0:T(8,128)} %fusion.4, f32[32,3,9119]{2,0,1:T(8,128)S(1)} %copy-done.5, f32[32,3,9120]{2,0,1:T(8,128)} %slice.255, f32[32,3,9215]{2,0,1:T(8,128)} %get-tuple-element.52), kind=kOutput, calls=%fused_computation.81 | convolution fusion | flops 683016192 | bytes 24743552 | tf_op jit(solution)/shard_map/kczn,jczn->kj/dot_general | solution.py:158
  224.4 53.0 %all-reduce.24 = (f32[64,32]{0,1:T(8,128)S(1)}, f32[64,32]{0,1:T(8,128)S(1)}) all-reduce(f32[64,32]{0,1:T(8,128)S(1)} %copy-done.20, f32[64,32]{0,1:T(8,128)S(1)} %fusion.48), channel_id=1, replica_groups=mesh['mesh'=16,'modes'=2] {'mesh'}, use_global_device_ids=true, to_apply=%region_1.2 | all-reduce | flops 4096 | bytes 32768 | tf_op jit(solution)/shard_map/psum | solution.py:160
  277.4 3.5 all_gather.10
  281.1 5.8 %cholesky.17 = f32[64,64]{1,0:T(8,128)S(1)} custom-call(f32[64,64]{1,0:T(8,128)S(1)} %fusion.61), custom_call_target="Cholesky" | custom-call | tf_op jit(solution)/shard_map/jit(cholesky)/cholesky | solution.py:132
  288.2 4.9 custom-call.7
  293.4 5.6 %bitcast_dynamic-update-slice_fusion.15 = (f32[8,32,3,9216]{3,1,2,0:T(8,128)S(1)}, f32[32,3,9216]{2,0,1:T(8,128)S(1)}) fusion(f32[64,3,1,9216]{3,0,1,2:T(8,128)} %all-gather.2.cloned.1.call-done, f32[64,64]{1,0:T(8,128)S(1)} %fusion.59, s32[]{:T(128)S(6)} %select_n.138), kind=kOutput, calls=%fused_computation.73 | convolution fusion | flops 679477248 | bytes 14172164 | tf_op jit(solution)/shard_map/kczn,kj->jczn/dot_general | solution.py:170
  299.0 4.9 collective-permute-start
  303.9 1.0 bitcast_dynamic-update-slice_fusion.14
  305.9 1.0 bitcast_dynamic-update-slice_fusion.12
  306.8 35.1 %collective-permute-done = f32[32,3,9216]{2,0,1:T(8,128)S(1)} collective-permute-done((f32[32,3,9216]{2,0,1:T(8,128)S(1)}, f32[32,3,9216]{2,0,1:T(8,128)S(1)}, u32[]{:S(2)}, u32[]{:S(2)}) %collective-permute-start) | collective-permute-done | bytes 3538976 | tf_op jit(solution)/shard_map/ppermute | solution.py:18
  342.2 1.0 bitcast_dynamic-update-slice_fusion.10
  344.2 1.0 bitcast_dynamic-update-slice_fusion.8
  345.1 9.3 %copy-done.2 = f32[8,32,3,9216]{3,1,2,0:T(8,128)} copy-done((f32[8,32,3,9216]{3,1,2,0:T(8,128)}, f32[8,32,3,9216]{3,1,2,0:T(8,128)S(1)}, u32[]{:S(2)}) %copy-start.2) | copy-done | bytes 28311576
  354.5 57.6 %fusion.6 = f32[32,9216,8,3]{1,2,3,0:T(8,128)S(1)} fusion(f32[8,3,8,3,1]{2,0,3,1,4:T(8,128)S(1)} %copy-done.14, f32[8,32,3,9216,1]{3,1,2,0,4:T(8,128)} %bitcast.199), kind=kOutput, calls=%fused_computation.8 | convolution fusion | flops 2038431744 | bytes 56625408 | tf_op jit(solution)/shard_map/acbd,bkdn->akcn/dot_general | solution.py:89
  412.1 18.7 %fusion.5 = f32[8,32,3,9216]{3,1,2,0:T(8,128)} fusion(f32[32,9216,8,3]{1,2,3,0:T(8,128)S(1)} %fusion.6, f32[9216]{0:T(1024)S(1)} %copy-done.12), kind=kLoop, calls=%fused_computation.7 | loop fusion | flops 7077888 | bytes 56659968 | tf_op jit(solution)/shard_map/mul | solution.py:89
  430.8 12.4 %slice_bitcast_fusion.14 = (f32[32,3,9216]{2,0,1:T(8,128)S(1)}, f32[32,3,9216]{2,0,1:T(8,128)S(1)}, f32[32,3,9216]{2,0,1:T(8,128)S(1)}, f32[32,3,9216]{2,0,1:T(8...) fusion(f32[8,32,3,9216]{3,1,2,0:T(8,128)} %fusion.5), kind=kLoop, calls=%fused_computation.50 | loop fusion | bytes 42467328 | tf_op jit(solution)/shard_map/squeeze | solution.py:93
  443.3 2.8 slice.240
  446.0 3.6 slice_select_fusion.6
  449.7 3.7 slice_select_fusion.7
  453.4 7.7 %fusion.29 = f32[32,3,9216]{2,0,1:T(8,128)} fusion(f32[8,32,3,9216]{3,1,2,0:T(8,128)} %fusion.5, f32[32,3,9119]{2,0,1:T(8,128)} %get-tuple-element.51, f32[32,3,9120]{2,0,1:T(8,128)} %slice.240, f32[32,3,9215]{2,0,1:T(8,128)} %get-tuple-element.49), kind=kLoop, calls=%fused_computation.45 | loop fusion | flops 2654208 | bytes 17620224 | tf_op jit(solution)/shard_map/add | solution.py:97
  461.0 1.9 collective-permute-start.1
  463.0 3.3 all_gather.11
  466.9 3.0 slice.231
  469.9 35.0 %collective-permute-done.1 = f32[32,3,9216]{2,0,1:T(8,128)} collective-permute-done((f32[32,3,9216]{2,0,1:T(8,128)}, f32[32,3,9216]{2,0,1:T(8,128)}, u32[]{:S(2)}, u32[]{:S(2)}) %collective-permute-start.1) | collective-permute-done | bytes 3538976 | tf_op jit(solution)/shard_map/ppermute | solution.py:18
  504.9 8.5 %fusion.35 = f32[32,3,1,9216]{3,0,1,2:T(8,128)} fusion(f32[32,3,9216]{2,0,1:T(8,128)} %collective-permute-done.1, f32[8,32,3,9216]{3,1,2,0:T(8,128)} %fusion.5, f32[32,3,9119]{2,0,1:T(8,128)S(1)} %get-tuple-element.50, f32[32,3,9120]{2,0,1:T(8,128)S(1)} %slice.231, f32[32,3,9215]{2,0,1:T(8,128)S(1)} %get-tuple-element.48, ...), kind=kOutput, calls=%fused_computation.57 | convolution fusion | flops 684785664 | bytes 28364804 | tf_op jit(solution)/shard_map/kczn,kj->jczn/dot_general | solution.py:171
  513.4 7.4 %copy.35 = f32[32,3,1,9216]{3,2,1,0:T(1,128)} copy(f32[32,3,1,9216]{3,0,1,2:T(8,128)} %fusion.35) | data formatting | bytes 7077888
  (71 shorter events, 8.4 us)
Async XLA Ops:
  7.2 170.9 %all-gather.2.cloned.1.call-start = ((), (), s32[]{:S(2)}) async-start(), calls=%async_computation | async-start | bytes 10616832 | tf_op jit(solution)/shard_map/all_gather | solution.py:157
  11.6 2.0 copy-start.1
  13.6 8.7 %copy-start.21 = (s32[1,9216]{1,0:T(1,128)S(1)}, s32[1,9216]{1,0:T(1,128)}, u32[]{:S(2)}) copy-start(s32[1,9216]{1,0:T(1,128)} %param.9) | copy-start | bytes 110596
  13.6 8.7 %copy-start.22 = (f32[16]{0:T(128)S(1)}, f32[16]{0:T(128)}, u32[]{:S(2)}) copy-start(f32[16]{0:T(128)} %param.10) | copy-start | bytes 196
  13.6 43.0 %collective-permute-start.2 = (f32[32,3,9216]{2,0,1:T(8,128)S(1)}, f32[32,3,9216]{2,0,1:T(8,128)S(1)}, u32[]{:S(2)}, u32[]{:S(2)}) collective-permute-start(f32[32,3,9216]{2,0,1:T(8,128)S(1)} %bitcast.186), channel_id=1, source_target_pairs={{0,2},{2,4},{4,6},{6,8},{8,10},{10,12},{12,14},{14,16},{16,18},{18... | collective-permute-start | bytes 10616840 | tf_op jit(solution)/shard_map/ppermute | solution.py:18
  22.6 1.0 copy-start.9
  23.6 103.8 %copy-start.11 = (f32[9216]{0:T(1024)}, f32[9216]{0:T(1024)S(1)}, u32[]{:S(2)}) copy-start(f32[9216]{0:T(1024)S(1)} %fusion.54) | copy-start | bytes 110596
  58.9 10.3 %copy-start.13 = (f32[8,3,8,3,1]{2,0,3,1,4:T(8,128)S(1)}, f32[8,3,8,3,1]{2,0,3,1,4:T(8,128)}, u32[]{:S(2)}) copy-start(f32[8,3,8,3,1]{2,0,3,1,4:T(8,128)} %constant.216) | copy-start | bytes 6916
  59.9 9.3 %copy-start.3 = (f32[8,32,3,9216]{3,1,2,0:T(8,128)}, f32[8,32,3,9216]{3,1,2,0:T(8,128)S(1)}, u32[]{:S(2)}) copy-start(f32[8,32,3,9216]{3,1,2,0:T(8,128)S(1)} %bitcast_dynamic-update-slice_fusion) | copy-start | bytes 84934656
  157.3 2.0 copy-start.8
  157.3 2.0 copy-start.18
  159.3 3.6 copy-start.16
  171.2 43.9 %collective-permute-start.3 = (f32[32,3,9216]{2,0,1:T(8,128)}, f32[32,3,9216]{2,0,1:T(8,128)}, u32[]{:S(2)}, u32[]{:S(2)}) collective-permute-start(f32[32,3,9216]{2,0,1:T(8,128)} %fusion.21), channel_id=1, source_target_pairs={{2,0},{4,2},{6,4},{8,6},{10,8},{12,10},{14,12},{16,14},{18,16},{20... | collective-permute-start | bytes 10616840 | tf_op jit(solution)/shard_map/ppermute | solution.py:18
  173.1 4.9 copy-start.4
  178.0 37.1 %copy-start = (f32[64,3,1,9216]{3,0,1,2:T(8,128)S(1)}, f32[64,3,1,9216]{3,0,1,2:T(8,128)}, u32[]{:S(2)}) copy-start(f32[64,3,1,9216]{3,0,1,2:T(8,128)} %all-gather.2.cloned.1.call-done) | copy-start | bytes 21233668
  178.0 37.1 %copy-start.5 = (f32[32,3,9119]{2,0,1:T(8,128)S(1)}, f32[32,3,9119]{2,0,1:T(8,128)}, u32[]{:S(2)}) copy-start(f32[32,3,9119]{2,0,1:T(8,128)} %get-tuple-element.54) | copy-start | bytes 10505092
  215.1 9.4 %copy-start.20 = (f32[64,32]{0,1:T(8,128)S(1)}, f32[64,32]{0,1:T(8,128)}, u32[]{:S(2)}) copy-start(f32[64,32]{0,1:T(8,128)} %fusion.43) | copy-start | bytes 24580
  299.0 42.9 %collective-permute-start = (f32[32,3,9216]{2,0,1:T(8,128)S(1)}, f32[32,3,9216]{2,0,1:T(8,128)S(1)}, u32[]{:S(2)}, u32[]{:S(2)}) collective-permute-start(f32[32,3,9216]{2,0,1:T(8,128)S(1)} %get-tuple-element.57), channel_id=1, source_target_pairs={{0,2},{2,4},{4,6},{6,8},{8,10},{10,12},{12,14},{14,16},{16,18},{18... | collective-permute-start | bytes 10616840 | tf_op jit(solution)/shard_map/ppermute | solution.py:18
  344.1 10.3 %copy-start.14 = (f32[8,3,8,3,1]{2,0,3,1,4:T(8,128)S(1)}, f32[8,3,8,3,1]{2,0,3,1,4:T(8,128)}, u32[]{:S(2)}) copy-start(f32[8,3,8,3,1]{2,0,3,1,4:T(8,128)} %constant.216) | copy-start | bytes 6916
  345.1 9.3 %copy-start.2 = (f32[8,32,3,9216]{3,1,2,0:T(8,128)}, f32[8,32,3,9216]{3,1,2,0:T(8,128)S(1)}, u32[]{:S(2)}) copy-start(f32[8,32,3,9216]{3,1,2,0:T(8,128)S(1)} %bitcast_dynamic-update-slice_fusion.8) | copy-start | bytes 84934656
  354.5 57.6 %copy-start.12 = (f32[9216]{0:T(1024)S(1)}, f32[9216]{0:T(1024)}, u32[]{:S(2)}) copy-start(f32[9216]{0:T(1024)} %copy-done.11) | copy-start | bytes 110596
  443.2 2.8 copy-start.7
  443.2 2.8 copy-start.19
  446.0 3.6 copy-start.6
  446.0 3.6 copy-start.17
  449.7 55.2 %slice-start = ((s8[7077888]{0:T(1024)(128)(4,1)}), s8[4194304]{0:T(1024)(128)(4,1)S(1)}, s32[]{:S(2)}) async-start(s8[7077888]{0:T(1024)(128)(4,1)} %bitcast.184), calls=%async_computation.1 | async-start | bytes 8388608
  453.3 51.5 %slice-start.1 = ((s8[7077888]{0:T(1024)(128)(4,1)}), s8[2883584]{0:T(1024)(128)(4,1)S(1)}, s32[]{:S(2)}) async-start(s8[7077888]{0:T(1024)(128)(4,1)} %bitcast.184), calls=%async_computation.2 | async-start | bytes 5767168
  461.0 43.8 %collective-permute-start.1 = (f32[32,3,9216]{2,0,1:T(8,128)}, f32[32,3,9216]{2,0,1:T(8,128)}, u32[]{:S(2)}, u32[]{:S(2)}) collective-permute-start(f32[32,3,9216]{2,0,1:T(8,128)} %fusion.29), channel_id=1, source_target_pairs={{2,0},{4,2},{6,4},{8,6},{10,8},{12,10},{14,12},{16,14},{18,16},{20... | collective-permute-start | bytes 10616840 | tf_op jit(solution)/shard_map/ppermute | solution.py:18
  466.6 3.3 copy-start.15
  466.9 38.0 %copy-start.10 = (f32[9216]{0:T(1024)S(1)}, f32[9216]{0:T(1024)}, u32[]{:S(2)}) copy-start(f32[9216]{0:T(1024)} %copy-done.9) | copy-start | bytes 110596
Sparse Core Ops, SparseCore 0:
  11.8 91.3 all-gather.1
where the time goes:
time: 534 us; the launch traced here: 528 us
  matrix products  149 us (28%)
  waiting for transfers between devices  130 us (24%)
  other arithmetic  84.4 us (16%)
  local copies, waits for them, and re-layouts  77.4 us (14%)
  blocking collectives  59.8 us (11%)
  between operations  14.7 us (3%)
  starting transfers between devices  13.4 us (3%)
    ppermute x4, waiting for transfers between devices, shifted(): return lax.ppermute(x, axis, pairs)  130 us
    dot_general x2, matrix products, layer_forces(): jnp.einsum('acbd,bkdn->akcn', element, stacked, precision=highest)  116 us
    psum x1, blocking collectives, per_device(): summed_stiff, summed_mass = lax.psum((tile_stiff, tile_mass), 'mesh')  53 us
    unnamed x59, local copies, waits for them, and re-layouts  40.7 us
    mul x2, other arithmetic, layer_forces(): jnp.einsum('acbd,bkdn->akcn', element, stacked, precision=highest)  37.3 us
    squeeze x2, local copies, waits for them, and re-layouts, layer_forces(): forces[corner]  23.7 us
    select_n x4, other arithmetic, shift_out(): moved = jnp.where(column >= 1, moved, 0.0)  14.6 us
    ppermute x4, starting transfers between devices, shifted(): return lax.ppermute(x, axis, pairs)  13.3 us
  transfers between devices with their start and end apart: 5, of which 4 were waited for; matrix products, arithmetic and copies ran while one was open for 25% of the time, Pallas kernels for 0%

commit v1 on v0

v1 whole, which is shorter than its diff:
```python
import functools

import jax
import jax.numpy as jnp
import numpy as np
from jax import lax
from jax.experimental import pallas as pl
from jax.experimental.pallas import tpu as pltpu
from jax.sharding import PartitionSpec as P

NX = 96
NY = 96


highest = lax.Precision.HIGHEST
high = lax.Precision.HIGH
MARGIN = 128
floor_modulus = 0.001


def shifted(x, axis, by):
    size = lax.axis_size(axis)
    pairs = [(i, i + by) for i in range(size) if 0 <= i + by < size]
    return lax.ppermute(x, axis, pairs)


def element_matrix():
    poisson_ratio = 0.3
    lame_first = poisson_ratio / ((1 + poisson_ratio) * (1 - 2 * poisson_ratio))
    shear_modulus = 1.0 / (2 * (1 + poisson_ratio))
    elastic = np.zeros((6, 6))
    elastic[:3, :3] = lame_first
    for normal_index in range(3):
        elastic[normal_index, normal_index] = lame_first + 2 * shear_modulus
        elastic[normal_index + 3, normal_index + 3] = shear_modulus
    corner_signs = [
        (1 - 2 * (corner & 1), 1 - 2 * (corner >> 1 & 1), 1 - 2 * (corner >> 2))
        for corner in range(8)
    ]
    gauss_point = 1.0 / np.sqrt(3.0)
    matrix = np.zeros((24, 24))
    for gauss_x in (-gauss_point, gauss_point):
        for gauss_y in (-gauss_point, gauss_point):
            for gauss_z in (-gauss_point, gauss_point):
                strain = np.zeros((6, 24))
                for corner in range(8):
                    sign_x, sign_y, sign_z = corner_signs[corner]
                    deriv_x = 2 * sign_x * (1 + sign_y * gauss_y) * (1 + sign_z * gauss_z) / 8
                    deriv_y = 2 * sign_y * (1 + sign_x * gauss_x) * (1 + sign_z * gauss_z) / 8
                    deriv_z = 2 * sign_z * (1 + sign_x * gauss_x) * (1 + sign_y * gauss_y) / 8
                    column = 3 * corner
                    strain[0, column] = deriv_x
                    strain[1, column + 1] = deriv_y
                    strain[2, column + 2] = deriv_z
                    strain[3, column] = deriv_y
                    strain[3, column + 1] = deriv_x
                    strain[4, column + 1] = deriv_z
                    strain[4, column + 2] = deriv_y
                    strain[5, column] = deriv_z
                    strain[5, column + 2] = deriv_x
                matrix = matrix + strain.T @ elastic @ strain / 8
    return matrix.reshape(8, 3, 8, 3)


def hadamard_matrix():
    signs = np.array([[1.0, 1.0], [1.0, -1.0]])
    transform = np.kron(np.kron(signs, signs), signs)
    matrix = np.einsum("ha,acbd,bg->hcgd", transform, element_matrix(), transform) / 64
    matrix[np.abs(matrix) < 1e-12] = 0.0
    return matrix


def layer_kernel(chunk, lanes_own, top_ref, bottom_ref, modulus_ref, inside_ref, out_top, out_bottom):
    matrix = hadamard_matrix()

    def step(index, carry):
        start = pl.multiple_of(index * chunk, 128)
        wide = chunk + 2 * MARGIN
        narrow = chunk + MARGIN
        inside = inside_ref[:, pl.ds(start, wide)]
        modulus = modulus_ref[:, pl.ds(start + MARGIN, narrow)]
        inside_narrow = inside[:, MARGIN:]
        hat = {}
        for c in range(3):
            top = top_ref[c, :, pl.ds(start, wide)]
            bottom = bottom_ref[c, :, pl.ds(start, wide)]
            for hz, plane in ((0, top + bottom), (1, top - bottom)):
                moved = pltpu.roll(plane, 1, 1) * inside
                for hx, line in ((0, plane + moved), (1, plane - moved)):
                    here = line[:, MARGIN:]
                    behind = pltpu.roll(line, NX, 1)[:, MARGIN:]
                    hat[hx + 4 * hz, c] = here + behind
                    hat[hx + 2 + 4 * hz, c] = here - behind

        def force(h, c):
            total = None
            for g in range(8):
                for d in range(3):
                    factor = float(matrix[h, c, g, d])
                    if factor != 0.0:
                        term = hat[g, d] * factor
                        total = term if total is None else total + term
            return None if total is None else total * modulus

        def both(first, second):
            if first is None:
                return second, -second
            return first + second, first - second

        for c in range(3):
            layers = []
            for hz in (0, 1):
                lines = []
                for hx in (0, 1):
                    near, far = both(force(hx + 4 * hz, c), force(hx + 2 + 4 * hz, c))
                    lines.append(near + pltpu.roll(far, narrow - NX, 1))
                near, far = both(lines[0], lines[1])
                layers.append((near + pltpu.roll(far * inside_narrow, narrow - 1, 1))[:, :chunk])
            out_top[c, :, pl.ds(start, chunk)] = layers[0] + layers[1]
            out_bottom[c, :, pl.ds(start, chunk)] = layers[0] - layers[1]
        return carry

    lax.fori_loop(0, lanes_own // chunk, step, 0)


def layer_forces(top, bottom, modulus, inside):
    comps, mode_count, wide = top.shape
    lanes_own = wide - 2 * MARGIN
    chunk = CHUNK if lanes_own % CHUNK == 0 else 128
    rows = 8
    in_block = pl.BlockSpec((comps, rows, wide), lambda m: (0, m, 0))
    row_block = pl.BlockSpec((1, wide), lambda m: (0, 0))
    out_block = pl.BlockSpec((comps, rows, lanes_own), lambda m: (0, m, 0))
    shape = jax.ShapeDtypeStruct((comps, mode_count, lanes_own), jnp.float32)
    return pl.pallas_call(
        functools.partial(layer_kernel, chunk, lanes_own),
        grid=(mode_count // rows,),
        in_specs=[in_block, in_block, row_block, row_block],
        out_specs=[out_block, out_block],
        out_shape=[shape, shape],
        cost_estimate=pl.CostEstimate(
            flops=240 * top.size, bytes_accessed=16 * top.size, transcendentals=0
        ),
        compiler_params=pltpu.CompilerParams(vmem_limit_bytes=32 * 2**20),
    )(top, bottom, modulus, inside)


CHUNK = 1152


def densities(classes, level_density):
    levels = level_density.shape[0]
    level_index = lax.iota(jnp.int32, levels).reshape(levels, 1, 1)
    matches = classes[None] == level_index
    return jnp.sum(jnp.where(matches, level_density[:, None, None], 0.0), 0)


def ritz_solve(gram_stiff, gram_mass):
    lower_factor = jnp.linalg.cholesky(gram_mass)
    identity = jnp.eye(gram_mass.shape[0], dtype=jnp.float32)
    inverse = jax.scipy.linalg.solve_triangular(lower_factor, identity, lower=True)
    rotate = inverse.T
    ritz_matrix = jnp.dot(
        jnp.dot(inverse, gram_stiff, precision=highest, preferred_element_type=jnp.float32),
        rotate,
        precision=highest,
        preferred_element_type=jnp.float32,
    )
    mixed_rotate = jnp.dot(
        rotate, ritz_matrix, precision=highest, preferred_element_type=jnp.float32
    )
    return (ritz_matrix, rotate, mixed_rotate)


def rotated(x, axis, by):
    size = lax.axis_size(axis)
    return lax.ppermute(x, axis, [(i, (i + by) % size) for i in range(size)])


def per_device(subspace, classes, level_density):
    mode_count, comps, plane_count, nodes = subspace.shape
    groups = lax.axis_size("modes")
    group = lax.axis_index("modes")
    total_dofs = comps * nodes * plane_count * lax.axis_size("mesh")
    lanes_own = nodes // groups
    wide = lanes_own + 2 * MARGIN

    density = densities(classes, level_density)
    modulus = floor_modulus + (1.0 - floor_modulus) * density * density * density
    own = group * lanes_own
    modulus = lax.dynamic_slice(jnp.pad(modulus, ((0, 0), (MARGIN, MARGIN))), (0, own), (1, wide))
    density = lax.dynamic_slice(density, (0, own), (1, lanes_own))
    inside = jnp.asarray(((np.arange(wide) - MARGIN) % NX >= 1)[None], jnp.float32)

    vectors = jnp.transpose(subspace[:, :, 0], (1, 0, 2))
    padded = jnp.pad(vectors, ((0, 0), (0, 0), (MARGIN, MARGIN)))
    tops, forces, bottoms = [], [], []
    for s in range(groups):
        target = lax.rem(group + s, groups)
        window = lax.dynamic_slice(
            padded, (0, 0, target * lanes_own), (comps, mode_count, wide)
        )
        top = window if s == 0 else rotated(window, "modes", s)
        tops.append(top)
        bottoms.append(shifted(top, "mesh", 1))
    for top, bottom in zip(tops, bottoms):
        forces.append(layer_forces(top, bottom, modulus, inside))
    returned = [shifted(force[1], "mesh", -1) for force in forces]
    middle = slice(MARGIN, MARGIN + lanes_own)
    top = jnp.concatenate([t[:, :, middle] for t in tops], 1)
    bottom = jnp.concatenate([b[:, :, middle] for b in bottoms], 1)
    force_top = jnp.concatenate([f[0] for f in forces], 1)
    force_bottom = jnp.concatenate([f[1] for f in forces], 1)
    mass = top * density

    def gram(a, b):
        return jnp.einsum("ckn,cjn->kj", a, b, precision=high)

    part_stiff = gram(top, force_top) + gram(bottom, force_bottom)
    part_mass = gram(top, mass)
    order = lax.rem(
        lax.rem(group - lax.iota(jnp.int32, groups) + groups, groups)[:, None] * mode_count
        + lax.iota(jnp.int32, mode_count)[None],
        groups * mode_count,
    ).reshape(-1)
    place = (order[:, None] == lax.iota(jnp.int32, groups * mode_count)[None]).astype(jnp.float32)

    def absolute(matrix):
        return jnp.dot(jnp.dot(place.T, matrix, precision=highest), place, precision=highest)

    def relative(matrix):
        return jnp.dot(jnp.dot(place, matrix, precision=highest), place.T, precision=highest)

    gram_stiff, gram_mass = lax.psum(
        (absolute(part_stiff), absolute(part_mass)), ("mesh", "modes")
    )
    ritz_matrix, rotate, mixed_rotate = ritz_solve(gram_stiff / total_dofs, gram_mass / total_dofs)
    rotate = relative(rotate)
    mixed_rotate = relative(mixed_rotate)
    image = force_top + jnp.concatenate(returned, 1)
    parts = []
    for s in reversed(range(groups)):
        columns = slice(s * mode_count, (s + 1) * mode_count)
        part = jnp.einsum("ckn,kj->jcn", image, rotate[:, columns], precision=high)
        part = part - jnp.einsum("ckn,kj->jcn", mass, mixed_rotate[:, columns], precision=high)
        parts.append(part if s == 0 else rotated(part, "modes", -s))
    parts = parts[::-1]
    residual = jnp.zeros((mode_count, comps, nodes), jnp.float32)
    for s, part in enumerate(parts):
        source = lax.rem(group + s, groups)
        residual = lax.dynamic_update_slice(residual, part, (0, 0, source * lanes_own))
    return (residual[:, :, None], ritz_matrix)


def solution(mesh):
    in_specs = (P("modes", None, "mesh", None), P("mesh", None), P())
    out_specs = (P("modes", None, "mesh", None), P())
    return jax.shard_map(
        per_device, mesh=mesh, in_specs=in_specs, out_specs=out_specs, check_vma=False
    )
```

time: 534 us -> 238 us (0.45)
  the two profiles are of different devices: /device:TPU:1 before, /device:TPU:0 now
where the time goes in v1:
time: 238 us; the launch traced here: 236 us
  waiting for transfers between devices  65.4 us (27%)
  blocking collectives  54.2 us (23%)
  Pallas kernels  38.3 us (16%)
  local copies, waits for them, and re-layouts  23.1 us (10%)
  matrix products  22.5 us (9%)
  other arithmetic  19.9 us (8%)
  starting transfers between devices  12 us (5%)
    ppermute x2, waiting for transfers between devices, rotated(): return lax.ppermute(x, axis, [(i, (i + by) % size) for i in range(size)])  65.4 us
    psum x1, blocking collectives, per_device(): lax.psum((absolute(part_stiff), absolute(part_mass)), ('mesh', 'modes'))  54.2 us
    pallas_call x2, Pallas kernels, layer_forces(): pl.pallas_call(functools.partial(layer_kernel, chunk, lanes_own), grid=(m...  38.3 us
    another operation x3, other arithmetic, ritz_solve(): lower_factor = jnp.linalg.cholesky(gram_mass)  8.6 us
    another operation x2, other arithmetic, ritz_solve(): jax.scipy.linalg.solve_triangular(lower_factor, identity, lower=True)  8.2 us
    dot_general x3, matrix products, gram(): return jnp.einsum('ckn,cjn->kj', a, b, precision=high)  6.79 us
    ppermute x4, starting transfers between devices, shifted(): return lax.ppermute(x, axis, pairs)  6.69 us
    dot_general x2, matrix products, per_device(): part = jnp.einsum('ckn,kj->jcn', image, rotate[:, columns], precision=high)  6.39 us
  transfers between devices with their start and end apart: 6, of which 2 were waited for; matrix products, arithmetic and copies ran while one was open for 21% of the time, Pallas kernels for 16%

profile of v1, /device:TPU:0, one launch (start us, length us, event | category | flops | bytes accessed | tf_op | source)
XLA Modules:
  0.0 236.5 jit_solution(16827703148216027542)
XLA Ops:
  0.6 4.4 %copy.20 = f32[32,3,1,9216]{3,0,1,2:T(8,128)} copy(f32[32,3,1,9216]{3,2,1,0:T(1,128)} %param.4) | data formatting | bytes 7077888 | tf_op args[0]
  5.1 3.7 %pad_dynamic-slice_fusion.2 = (f32[3,32,4864]{2,1,0:T(8,128)S(1)}, f32[3,32,4864]{2,1,0:T(8,128)}) fusion(s32[]{:T(128)S(6)} %select_n.34, f32[3,32,9216]{2,1,0:T(8,128)} %bitcast.53, s32[]{:T(128)S(6)} %select_n.35), kind=kLoop, calls=%fused_computation.21 | loop fusion | bytes 7274504 | tf_op jit(solution)/shard_map/dynamic_slice | solution.py:200
  8.7 3.0 %collective-permute-start = (f32[3,32,4864]{2,1,0:T(8,128)}, f32[3,32,4864]{2,1,0:T(8,128)}, u32[]{:S(2)}, u32[]{:S(2)}) collective-permute-start(f32[3,32,4864]{2,1,0:T(8,128)} %get-tuple-element.13), channel_id=1, source_target_pairs={{0,1},{1,0},{2,3},{3,2},{4,5},{5,4},{6,7},{7,6},{8,9},{9,8},{10,11... | collective-permute-start | bytes 5603336 | tf_op jit(solution)/shard_map/ppermute | solution.py:177
  11.7 2.7 %collective-permute-start.1 = (f32[3,32,4864]{2,1,0:T(8,128)S(1)}, f32[3,32,4864]{2,1,0:T(8,128)}, u32[]{:S(2)}, u32[]{:S(2)}) collective-permute-start(f32[3,32,4864]{2,1,0:T(8,128)S(1)} %get-tuple-element.12.top_ref), channel_id=1, source_target_pairs={{0,2},{2,4},{4,6},{6,8},{8,10},{10,12},{12,14},{14,16},{16,18},{18... | collective-permute-start | bytes 5603336 | tf_op jit(solution)/shard_map/ppermute | solution.py:24
  14.4 0.2 select_reduce_fusion
  14.9 1.6 pad_dynamic-slice_fusion
  16.6 36.1 %collective-permute-done.top_ref = f32[3,32,4864]{2,1,0:T(8,128)} collective-permute-done((f32[3,32,4864]{2,1,0:T(8,128)}, f32[3,32,4864]{2,1,0:T(8,128)}, u32[]{:S(2)}, u32[]{:S(2)}) %collective-permute-start) | collective-permute-done | bytes 1867808 | tf_op jit(solution)/shard_map/ppermute | solution.py:177
  52.7 1.4 collective-permute-start.2
  54.2 19.5 %shard_map.62 = (f32[3,32,4608]{2,1,0:T(8,128)S(1)}, f32[3,32,4608]{2,1,0:T(8,128)}) custom-call(f32[3,32,4864]{2,1,0:T(8,128)S(1)} %get-tuple-element.12.top_ref, f32[3,32,4864]{2,1,0:T(8,128)} %collective-permute-done.1.bottom_ref, f32[1,4864]{1,0:T(1,128)S(1)} %pad_dynamic-slice_fusion.3.modulus_ref, f32[1,4864]{1,0:T(1,128)S(1)} %copy-done), custom_call_target="tpu_custom_call" | custom-call | flops 112066560 | bytes 7471104 | tf_op jit(solution)/shard_map/pallas_call | solution.py:135
  73.7 1.3 collective-permute-start.3
  75.0 1.6 slice.44
  76.6 2.2 slice.46
  78.8 1.6 fusion.24
  80.5 0.3 fusion.46
  80.7 0.9 fusion.45
  81.8 18.8 %shard_map.63 = (f32[3,32,4608]{2,1,0:T(8,128)S(1)}, f32[3,32,4608]{2,1,0:T(8,128)S(1)}) custom-call(f32[3,32,4864]{2,1,0:T(8,128)} %collective-permute-done.top_ref, f32[3,32,4864]{2,1,0:T(8,128)S(1)} %collective-permute-done.2.bottom_ref, f32[1,4864]{1,0:T(1,128)S(1)} %pad_dynamic-slice_fusion.3.modulus_ref, f32[1,4864]{1,0:T(1,128)S(1)} %copy-done), custom_call_target="tpu_custom_call" | custom-call | flops 112066560 | bytes 7471104 | tf_op jit(solution)/shard_map/pallas_call | solution.py:135
  100.6 1.3 collective-permute-start.4
  102.1 1.8 fusion.18
  104.1 3.4 %fusion.27 = f32[64,64]{1,0:T(8,128)S(1)} fusion(f32[64,64]{1,0:T(8,128)S(1)} %fusion.18, f32[3,32,4608]{2,1,0:T(8,128)S(1)} %get-tuple-element.9, f32[3,32,4608]{2,1,0:T(8,128)} %get-tuple-element.8, f32[3,32,4608]{2,1,0:T(8,128)S(1)} %slice.47, f32[3,32,4608]{2,1,0:T(8,128)S(1)} %slice.46), kind=kOutput, calls=%fused_computation.33 | convolution fusion | flops 341512192 | bytes 7110656 | tf_op jit(solution)/shard_map/ckn,cjn->kj/dot_general | solution.py:217
  107.4 0.3 fusion.42
  107.7 0.9 fusion.41
  108.6 54.2 %all-reduce.2 = (f32[64,64]{0,1:T(8,128)}, f32[64,64]{0,1:T(8,128)}) all-reduce(f32[64,64]{0,1:T(8,128)} %fusion.45, f32[64,64]{0,1:T(8,128)} %fusion.41), channel_id=1, replica_groups=mesh['mesh'=16,'modes'=2] {'mesh','modes'}, use_global_device_ids=true, to_apply=%region_1.2 | all-reduce | flops 8192 | bytes 65536 | tf_op jit(solution)/shard_map/psum | solution.py:234
  162.8 1.4 broadcast_multiply_fusion
  164.2 1.4 copy.13
  165.6 1.4 fusion.36
  167.0 7.2 %cholesky.17 = f32[64,64]{1,0:T(8,128)} custom-call(f32[64,64]{1,0:T(8,128)} %fusion.36), custom_call_target="Cholesky" | custom-call | tf_op jit(solution)/shard_map/jit(cholesky)/cholesky | solution.py:159
  174.3 0.8 select_reduce_fusion.1
  175.0 0.6 compare_reduce_fusion
  175.6 1.9 fusion.33
  177.6 6.3 %custom-call.7 = f32[1,64,64]{1,2,0:T(8,128)} custom-call(f32[1,64,64]{2,1,0:T(8,128)} %fusion.33), custom_call_target="InvertDiagBlocksLowerTriangular" | custom-call | tf_op jit(solution)/shard_map/jit(_solve_triangular)/triangular_solve | solution.py:161
  183.8 1.1 fusion.34
  185.0 0.2 fusion.44
  185.2 0.2 fusion.43
  185.4 0.9 fusion.37
  186.4 0.2 fusion.67
  186.6 0.2 fusion.68
  186.8 0.2 fusion.40
  187.0 0.2 fusion.39
  187.3 2.5 %fusion.1 = f32[32,3,4608]{2,0,1:T(8,128)S(1)} fusion(f32[4608]{0:T(1024)} %copy-done.8, f32[3,32,4608]{2,1,0:T(8,128)} %copy-done.3, f32[3,32,4608]{2,1,0:T(8,128)S(1)} %copy-done.2, f32[64,64]{0,1:T(8,128)S(1)} %fusion.39), kind=kOutput, calls=%fused_computation.3 | convolution fusion | flops 171638784 | bytes 5343232 | tf_op jit(solution)/shard_map/ckn,kj->jcn/dot_general | solution.py:245
  189.9 3.3 %convolution_subtract_fusion = f32[32,3,4608]{2,0,1:T(8,128)S(1)} fusion(f32[32,3,4608]{2,0,1:T(8,128)S(1)} %fusion.1, f32[3,64,4608]{2,1,0:T(8,128)S(1)} %copy-done.6, f32[3,32,4608]{2,1,0:T(8,128)} %collective-permute-done.4, f32[3,32,4608]{2,1,0:T(8,128)} %collective-permute-done.3, f32[64,64]{0,1:T(8,128)S(1)} %fusion.43), kind=kOutput, calls=%fused_computation | convolution fusion | flops 172081152 | bytes 10633216 | tf_op jit(solution)/shard_map/ckn,kj->jcn/dot_general | solution.py:244
  193.1 2.3 collective-permute-start.5
  195.5 1.1 fusion.3
  196.5 3.1 %fusion = f32[32,3,1,4608]{3,0,1,2:T(8,128)S(1)} fusion(f32[32,3,4608]{2,0,1:T(8,128)S(1)} %fusion.3, f32[3,64,4608]{2,1,0:T(8,128)S(1)} %copy-done.6, f32[3,32,4608]{2,1,0:T(8,128)} %collective-permute-done.4, f32[3,32,4608]{2,1,0:T(8,128)} %collective-permute-done.3, f32[64,64]{0,1:T(8,128)S(1)} %fusion.43), kind=kOutput, calls=%fused_computation.2 | convolution fusion | flops 172081152 | bytes 10633216 | tf_op jit(solution)/shard_map/ckn,kj->jcn/dot_general | solution.py:244
  199.7 1.8 broadcast_in_dim.28
  201.5 2.0 copy_dynamic-update-slice_fusion.1
  203.5 29.3 %collective-permute-done.5 = f32[32,3,4608]{2,0,1:T(8,128)S(1)} collective-permute-done((f32[32,3,4608]{2,0,1:T(8,128)S(1)}, f32[32,3,4608]{2,0,1:T(8,128)S(1)}, u32[]{:S(2)}, u32[]{:S(2)}) %collective-permute-start.5) | collective-permute-done | bytes 1769504 | tf_op jit(solution)/shard_map/ppermute | solution.py:177
  232.7 1.9 copy_dynamic-update-slice_fusion
  234.7 1.8 copy-done.7
  (39 shorter events, 0.8 us)
Async XLA Ops:
  5.0 9.4 %copy-start.11 = (s32[1,9216]{1,0:T(1,128)S(1)}, s32[1,9216]{1,0:T(1,128)}, u32[]{:S(2)}) copy-start(s32[1,9216]{1,0:T(1,128)} %param.5) | copy-start | bytes 110596
  5.1 9.4 %copy-start.12 = (f32[16]{0:T(128)S(1)}, f32[16]{0:T(128)}, u32[]{:S(2)}) copy-start(f32[16]{0:T(128)} %param.6) | copy-start | bytes 196
  8.7 45.4 %copy-start = (f32[1,4864]{1,0:T(1,128)S(1)}, f32[1,4864]{1,0:T(1,128)}, u32[]{:S(2)}) copy-start(f32[1,4864]{1,0:T(1,128)} %constant.87.clone.inside_ref) | copy-start | bytes 58372
  8.7 44.0 %collective-permute-start = (f32[3,32,4864]{2,1,0:T(8,128)}, f32[3,32,4864]{2,1,0:T(8,128)}, u32[]{:S(2)}, u32[]{:S(2)}) collective-permute-start(f32[3,32,4864]{2,1,0:T(8,128)} %get-tuple-element.13), channel_id=1, source_target_pairs={{0,1},{1,0},{2,3},{3,2},{4,5},{5,4},{6,7},{7,6},{8,9},{9,8},{10,11... | collective-permute-start | bytes 5603336 | tf_op jit(solution)/shard_map/ppermute | solution.py:177
  11.7 42.5 %collective-permute-start.1 = (f32[3,32,4864]{2,1,0:T(8,128)S(1)}, f32[3,32,4864]{2,1,0:T(8,128)}, u32[]{:S(2)}, u32[]{:S(2)}) collective-permute-start(f32[3,32,4864]{2,1,0:T(8,128)S(1)} %get-tuple-element.12.top_ref), channel_id=1, source_target_pairs={{0,2},{2,4},{4,6},{6,8},{8,10},{10,12},{12,14},{14,16},{16,18},{18... | collective-permute-start | bytes 5603336 | tf_op jit(solution)/shard_map/ppermute | solution.py:24
  14.9 65.5 %copy-start.8 = (f32[4608]{0:T(1024)}, f32[4608]{0:T(1024)S(1)}, u32[]{:S(2)}) copy-start(f32[4608]{0:T(1024)S(1)} %dynamic-slice.3) | copy-start | bytes 55300
  16.6 85.5 %copy-start.1 = (f32[3,32,4608]{2,1,0:T(8,128)}, f32[3,32,4608]{2,1,0:T(8,128)S(1)}, u32[]{:S(2)}) copy-start(f32[3,32,4608]{2,1,0:T(8,128)S(1)} %pad_dynamic-slice_fusion) | copy-start | bytes 5308420
  52.7 29.1 %collective-permute-start.2 = (f32[3,32,4864]{2,1,0:T(8,128)}, f32[3,32,4864]{2,1,0:T(8,128)S(1)}, u32[]{:S(2)}, u32[]{:S(2)}) collective-permute-start(f32[3,32,4864]{2,1,0:T(8,128)} %collective-permute-done.top_ref), channel_id=1, source_target_pairs={{0,2},{2,4},{4,6},{6,8},{8,10},{10,12},{12,14},{14,16},{16,18},{18... | collective-permute-start | bytes 5603336 | tf_op jit(solution)/shard_map/ppermute | solution.py:24
  73.7 116.2 %collective-permute-start.3 = (f32[3,32,4608]{2,1,0:T(8,128)}, f32[3,32,4608]{2,1,0:T(8,128)}, u32[]{:S(2)}, u32[]{:S(2)}) collective-permute-start(f32[3,32,4608]{2,1,0:T(8,128)} %get-tuple-element.8), channel_id=1, source_target_pairs={{2,0},{4,2},{6,4},{8,6},{10,8},{12,10},{14,12},{16,14},{18,16},{20... | collective-permute-start | bytes 5308424 | tf_op jit(solution)/shard_map/ppermute | solution.py:24
  76.5 25.5 %copy-start.3 = (f32[3,32,4608]{2,1,0:T(8,128)}, f32[3,32,4608]{2,1,0:T(8,128)S(1)}, u32[]{:S(2)}) copy-start(f32[3,32,4608]{2,1,0:T(8,128)S(1)} %slice.44) | copy-start | bytes 5308420
  100.6 89.2 %collective-permute-start.4 = (f32[3,32,4608]{2,1,0:T(8,128)S(1)}, f32[3,32,4608]{2,1,0:T(8,128)}, u32[]{:S(2)}, u32[]{:S(2)}) collective-permute-start(f32[3,32,4608]{2,1,0:T(8,128)S(1)} %get-tuple-element.9), channel_id=1, source_target_pairs={{2,0},{4,2},{6,4},{8,6},{10,8},{12,10},{14,12},{16,14},{18,16},{20... | collective-permute-start | bytes 5308424 | tf_op jit(solution)/shard_map/ppermute | solution.py:24
  102.1 1.8 copy-start.5
  104.1 83.2 %copy-start.2 = (f32[3,32,4608]{2,1,0:T(8,128)S(1)}, f32[3,32,4608]{2,1,0:T(8,128)}, u32[]{:S(2)}) copy-start(f32[3,32,4608]{2,1,0:T(8,128)} %copy-done.1) | copy-start | bytes 5308420
  183.8 6.0 %copy-start.6 = (f32[3,64,4608]{2,1,0:T(8,128)S(1)}, f32[3,64,4608]{2,1,0:T(8,128)}, u32[]{:S(2)}) copy-start(f32[3,64,4608]{2,1,0:T(8,128)} %copy-done.5) | copy-start | bytes 10616836
  186.6 6.6 %copy-start.10 = (f32[64,64]{1,0:T(8,128)}, f32[64,64]{1,0:T(8,128)S(1)}, u32[]{:S(2)}) copy-start(f32[64,64]{1,0:T(8,128)S(1)} %fusion.67) | copy-start | bytes 49156
  189.8 5.7 %copy-start.4 = (f32[3,32,4608]{2,1,0:T(8,128)S(1)}, f32[3,32,4608]{2,1,0:T(8,128)}, u32[]{:S(2)}) copy-start(f32[3,32,4608]{2,1,0:T(8,128)} %copy-done.3) | copy-start | bytes 5308420
  189.8 5.7 %copy-start.9 = (f32[4608]{0:T(1024)S(1)}, f32[4608]{0:T(1024)}, u32[]{:S(2)}) copy-start(f32[4608]{0:T(1024)} %copy-done.8) | copy-start | bytes 55300
  193.1 39.6 %collective-permute-start.5 = (f32[32,3,4608]{2,0,1:T(8,128)S(1)}, f32[32,3,4608]{2,0,1:T(8,128)S(1)}, u32[]{:S(2)}, u32[]{:S(2)}) collective-permute-start(f32[32,3,4608]{2,0,1:T(8,128)S(1)} %convolution_subtract_fusion), channel_id=1, source_target_pairs={{0,1},{1,0},{2,3},{3,2},{4,5},{5,4},{6,7},{7,6},{8,9},{9,8},{10,11... | collective-permute-start | bytes 5308424 | tf_op jit(solution)/shard_map/ppermute | solution.py:177
  234.7 1.8 copy-start.7

commit v2 on v1

--- a/solution.py
+++ b/solution.py
@@ -126,7 +126,7 @@
 def layer_forces(top, bottom, modulus, inside):
     comps, mode_count, wide = top.shape
     lanes_own = wide - 2 * MARGIN
-    chunk = CHUNK if lanes_own % CHUNK == 0 else 128
+    chunk = next(size for size in CHUNKS if lanes_own % size == 0)
     rows = 8
     in_block = pl.BlockSpec((comps, rows, wide), lambda m: (0, m, 0))
     row_block = pl.BlockSpec((1, wide), lambda m: (0, 0))
@@ -145,7 +145,7 @@
     )(top, bottom, modulus, inside)
 
 
-CHUNK = 1152
+CHUNKS = (2304, 1152, 384, 128)
 
 
 def densities(classes, level_density):
@@ -155,21 +155,107 @@
     return jnp.sum(jnp.where(matches, level_density[:, None, None], 0.0), 0)
 
 
-def ritz_solve(gram_stiff, gram_mass):
-    lower_factor = jnp.linalg.cholesky(gram_mass)
-    identity = jnp.eye(gram_mass.shape[0], dtype=jnp.float32)
-    inverse = jax.scipy.linalg.solve_triangular(lower_factor, identity, lower=True)
-    rotate = inverse.T
-    ritz_matrix = jnp.dot(
-        jnp.dot(inverse, gram_stiff, precision=highest, preferred_element_type=jnp.float32),
-        rotate,
-        precision=highest,
+def dot(a, b, contract):
+    return lax.dot_general(
+        a, b, ((contract[:1], contract[1:]), ((), ())), precision=highest,
         preferred_element_type=jnp.float32,
     )
-    mixed_rotate = jnp.dot(
-        rotate, ritz_matrix, precision=highest, preferred_element_type=jnp.float32
-    )
-    return (ritz_matrix, rotate, mixed_rotate)
+
+
+def ritz_kernel(
+    axes, mode_count, total_dofs, stiff_ref, mass_ref, ritz_ref, rotate_ref, mixed_ref,
+    sums, landed, send_sem, recv_sem,
+):
+    size = stiff_ref.shape[0]
+    groups = size // mode_count
+    partners = []
+    for name, count in axes:
+        own = lax.axis_index(name)
+        bit = 1
+        while bit < count:
+            set_here = lax.rem(lax.div(own, bit), 2)
+            partners.append({name: own + bit - 2 * bit * set_here})
+            bit *= 2
+    barrier = pltpu.get_barrier_semaphore()
+    for partner in partners:
+        pl.semaphore_signal(
+            barrier, inc=1, device_id=partner, device_id_type=pl.DeviceIdType.MESH
+        )
+
+    group = lax.axis_index("modes")
+    row = lax.broadcasted_iota(jnp.int32, (size, size), 0)
+    column = lax.broadcasted_iota(jnp.int32, (size, size), 1)
+    place = jnp.zeros((size, size), jnp.float32)
+    for s in range(groups):
+        move = (lax.rem(group - s + groups, groups) - s) * mode_count
+        here = (row >= s * mode_count) & (row < (s + 1) * mode_count) & (column - row == move)
+        place = jnp.where(here, 1.0, place)
+
+    sums[0, :, :size] = dot(dot(place, stiff_ref[...], (0, 0)), place, (1, 0))
+    sums[0, :, size:] = dot(dot(place, mass_ref[...], (0, 0)), place, (1, 0))
+    pl.semaphore_wait(barrier, len(partners))
+    for step, partner in enumerate(partners):
+        copy = pltpu.make_async_remote_copy(
+            src_ref=sums.at[step],
+            dst_ref=landed.at[step],
+            send_sem=send_sem.at[step],
+            recv_sem=recv_sem.at[step],
+            device_id=partner,
+            device_id_type=pl.DeviceIdType.MESH,
+        )
+        copy.start()
+        copy.wait()
+        sums[step + 1] = sums[step] + landed[step]
+    total = sums[len(partners)] * (1.0 / total_dofs)
+    gram_stiff = total[:, :size]
+
+    lane = lax.broadcasted_iota(jnp.int32, (8, 2 * size), 1)
+    sub = lax.broadcasted_iota(jnp.int32, (8, 2 * size), 0)
+    blocks = []
+    for block in range(size // 8):
+        unit = jnp.where(lane == sub + 8 * block, 1.0, 0.0)
+        blocks.append(jnp.where(lane < size, unit, total[8 * block : 8 * block + 8]))
+    for k in range(size):
+        at = k // 8
+        pivot_row = blocks[at][k % 8 : k % 8 + 1]
+        pivot_row = pivot_row / pivot_row[:, size + k : size + k + 1]
+        for block in range(at, size // 8):
+            factor = blocks[block][:, size + k : size + k + 1]
+            if block == at:
+                factor = jnp.where(sub[:, :1] > k % 8, factor, 0.0)
+            blocks[block] = blocks[block] - factor * pivot_row
+    rows = jnp.concatenate(blocks, 0)
+    row = lax.broadcasted_iota(jnp.int32, (size, 2 * size), 0)
+    column = lax.broadcasted_iota(jnp.int32, (size, 2 * size), 1)
+    pivots = jnp.sum(jnp.where(column == row + size, rows, 0.0), 1, keepdims=True)
+    inverse = rows[:, :size] * (1.0 / jnp.sqrt(pivots))
+    ritz = dot(dot(inverse, gram_stiff, (1, 0)), inverse, (1, 1))
+    ritz_ref[...] = ritz
+    mixed = dot(ritz, inverse, (0, 0))
+    rotate_ref[...] = dot(dot(place, inverse, (1, 0)), place, (1, 1))
+    mixed_ref[...] = dot(dot(place, mixed, (1, 0)), place, (1, 1))
+
+
+def ritz_solve(part_stiff, part_mass, mode_count, total_dofs):
+    size = part_stiff.shape[0]
+    axes = [(name, lax.axis_size(name)) for name in ("mesh", "modes")]
+    steps = sum(count.bit_length() - 1 for name, count in axes)
+    shape = jax.ShapeDtypeStruct((size, size), jnp.float32)
+    whole = pl.BlockSpec(memory_space=pltpu.VMEM)
+    return pl.pallas_call(
+        functools.partial(ritz_kernel, axes, mode_count, total_dofs),
+        in_specs=[whole, whole],
+        out_specs=[whole] * 3,
+        out_shape=[shape] * 3,
+        scratch_shapes=[
+            pltpu.VMEM((steps + 1, size, 2 * size), jnp.float32),
+            pltpu.VMEM((steps, size, 2 * size), jnp.float32),
+            pltpu.SemaphoreType.DMA((steps,)),
+            pltpu.SemaphoreType.DMA((steps,)),
+        ],
+        cost_estimate=pl.CostEstimate(flops=10**7, bytes_accessed=10**5, transcendentals=0),
+        compiler_params=pltpu.CompilerParams(collective_id=0, has_side_effects=True),
+    )(part_stiff, part_mass)
 
 
 def rotated(x, axis, by):
@@ -218,31 +304,13 @@
 
     part_stiff = gram(top, force_top) + gram(bottom, force_bottom)
     part_mass = gram(top, mass)
-    order = lax.rem(
-        lax.rem(group - lax.iota(jnp.int32, groups) + groups, groups)[:, None] * mode_count
-        + lax.iota(jnp.int32, mode_count)[None],
-        groups * mode_count,
-    ).reshape(-1)
-    place = (order[:, None] == lax.iota(jnp.int32, groups * mode_count)[None]).astype(jnp.float32)
-
-    def absolute(matrix):
-        return jnp.dot(jnp.dot(place.T, matrix, precision=highest), place, precision=highest)
-
-    def relative(matrix):
-        return jnp.dot(jnp.dot(place, matrix, precision=highest), place.T, precision=highest)
-
-    gram_stiff, gram_mass = lax.psum(
-        (absolute(part_stiff), absolute(part_mass)), ("mesh", "modes")
-    )
-    ritz_matrix, rotate, mixed_rotate = ritz_solve(gram_stiff / total_dofs, gram_mass / total_dofs)
-    rotate = relative(rotate)
-    mixed_rotate = relative(mixed_rotate)
+    ritz_matrix, rotate, mixed_rotate = ritz_solve(part_stiff, part_mass, mode_count, total_dofs)
     image = force_top + jnp.concatenate(returned, 1)
     parts = []
     for s in reversed(range(groups)):
         columns = slice(s * mode_count, (s + 1) * mode_count)
-        part = jnp.einsum("ckn,kj->jcn", image, rotate[:, columns], precision=high)
-        part = part - jnp.einsum("ckn,kj->jcn", mass, mixed_rotate[:, columns], precision=high)
+        part = jnp.einsum("ckn,jk->jcn", image, rotate[columns], precision=high)
+        part = part - jnp.einsum("ckn,jk->jcn", mass, mixed_rotate[columns], precision=high)
         parts.append(part if s == 0 else rotated(part, "modes", -s))
     parts = parts[::-1]
     residual = jnp.zeros((mode_count, comps, nodes), jnp.float32)

time: 238 us -> 181 us (0.76)
  blocking collectives: 54.2 us -> 0 us
  Pallas kernels: 38.3 us -> 62.8 us
  other arithmetic: 19.9 us -> 0.25 us
  matrix products: 22.5 us -> 18.1 us
    psum x1 -> x0, blocking collectives: 54.2 us -> none  [per_device(): lax.psum((absolute(part_stiff), absolute(part_mass)), ('mesh', 'modes'))]
    pallas_call x0 -> x1, Pallas kernels: none -> 33.7 us  [ritz_solve(): pl.pallas_call(functools.partial(ritz_kernel, axes, mode_count, total_dof...]
    another operation x5 -> x0, other arithmetic: 16.8 us -> none  [the longest x3 8.6 us: ritz_solve(): lower_factor = jnp.linalg.cholesky(gram_mass)]
    pallas_call x2, Pallas kernels: 38.3 us -> 29 us  [layer_forces(): pl.pallas_call(functools.partial(layer_kernel, chunk, lanes_own), grid=(m...]
    dot_general x15 -> x4, matrix products: 14.6 us -> 10.1 us  [the longest x2 6.4 us: per_device(): part = jnp.einsum('ckn,jk->jcn', image, rotate[columns], precision=high)]
    div x2 -> x0, other arithmetic: 2.76 us -> none  [the longest x1 1.4 us: ritz_solve(): lower_factor = jnp.linalg.cholesky(gram_mass)]
    unnamed x28 -> x33, local copies, waits for them, and re-layouts: 6.36 us -> 6.44 us
  transfers between devices with their start and end apart: 6 -> 6, of which waited for: 2 -> 2; matrix products, arithmetic and copies ran while one was open for 21% -> 15% of each run, Pallas kernels for 16% -> 35%
where the time goes in v2:
time: 181 us; the launch traced here: 180 us
  waiting for transfers between devices  64.6 us (36%)
  Pallas kernels  62.8 us (35%)
  local copies, waits for them, and re-layouts  21.9 us (12%)
  matrix products  18.1 us (10%)
  starting transfers between devices  11.5 us (6%)
    ppermute x2, waiting for transfers between devices, rotated(): return lax.ppermute(x, axis, [(i, (i + by) % size) for i in range(size)])  64.6 us
    pallas_call x1, Pallas kernels, ritz_solve(): pl.pallas_call(functools.partial(ritz_kernel, axes, mode_count, total_dof...  33.7 us
    pallas_call x2, Pallas kernels, layer_forces(): pl.pallas_call(functools.partial(layer_kernel, chunk, lanes_own), grid=(m...  29 us
    ppermute x4, starting transfers between devices, shifted(): return lax.ppermute(x, axis, pairs)  8 us
    dot_general x3, matrix products, gram(): return jnp.einsum('ckn,cjn->kj', a, b, precision=high)  7.91 us
    unnamed x33, local copies, waits for them, and re-layouts  6.44 us
    dot_general x2, matrix products, per_device(): part = jnp.einsum('ckn,jk->jcn', image, rotate[columns], precision=high)  6.4 us
    dynamic_update_slice x2, local copies, waits for them, and re-layouts, per_device(): lax.dynamic_update_slice(residual, part, (0, 0, source * lanes_own))  3.9 us
  transfers between devices with their start and end apart: 6, of which 2 were waited for; matrix products, arithmetic and copies ran while one was open for 15% of the time, Pallas kernels for 35%

profile of v2, /device:TPU:0, one launch (start us, length us, event | category | flops | bytes accessed | tf_op | source)
XLA Modules:
  0.0 180.1 jit_solution(7490220629846921185)
XLA Ops:
  0.6 4.4 %copy.15 = f32[32,3,1,9216]{3,0,1,2:T(8,128)} copy(f32[32,3,1,9216]{3,2,1,0:T(1,128)} %param.4) | data formatting | bytes 7077888 | tf_op args[0]
  5.1 2.3 %pad_dynamic-slice_fusion.2 = (f32[3,32,4864]{2,1,0:T(8,128)S(1)}, f32[3,32,4864]{2,1,0:T(8,128)S(1)}) fusion(s32[]{:T(128)S(6)} %select_n.30, f32[3,32,9216]{2,1,0:T(8,128)} %bitcast.31, s32[]{:T(128)S(6)} %select_n.31), kind=kLoop, calls=%fused_computation.21 | loop fusion | bytes 7274504 | tf_op jit(solution)/shard_map/dynamic_slice | solution.py:286
  7.3 0.0 copy-start
  7.4 3.0 %collective-permute-start = (f32[3,32,4864]{2,1,0:T(8,128)S(1)}, f32[3,32,4864]{2,1,0:T(8,128)}, u32[]{:S(2)}, u32[]{:S(2)}) collective-permute-start(f32[3,32,4864]{2,1,0:T(8,128)S(1)} %get-tuple-element.17), channel_id=1, source_target_pairs={{0,1},{1,0},{2,3},{3,2},{4,5},{5,4},{6,7},{7,6},{8,9},{9,8},{10,11... | collective-permute-start | bytes 5603336 | tf_op jit(solution)/shard_map/ppermute | solution.py:263
  10.4 2.7 %collective-permute-start.1 = (f32[3,32,4864]{2,1,0:T(8,128)S(1)}, f32[3,32,4864]{2,1,0:T(8,128)}, u32[]{:S(2)}, u32[]{:S(2)}) collective-permute-start(f32[3,32,4864]{2,1,0:T(8,128)S(1)} %get-tuple-element.16.top_ref), channel_id=1, source_target_pairs={{0,2},{2,4},{4,6},{6,8},{8,10},{10,12},{12,14},{14,16},{16,18},{18... | collective-permute-start | bytes 5603336 | tf_op jit(solution)/shard_map/ppermute | solution.py:24
  13.1 0.2 select_reduce_fusion
  13.3 37.9 %collective-permute-done.top_ref = f32[3,32,4864]{2,1,0:T(8,128)} collective-permute-done((f32[3,32,4864]{2,1,0:T(8,128)S(1)}, f32[3,32,4864]{2,1,0:T(8,128)}, u32[]{:S(2)}, u32[]{:S(2)}) %collective-permute-start) | collective-permute-done | bytes 1867808 | tf_op jit(solution)/shard_map/ppermute | solution.py:263
  51.2 2.6 %collective-permute-start.2 = (f32[3,32,4864]{2,1,0:T(8,128)}, f32[3,32,4864]{2,1,0:T(8,128)}, u32[]{:S(2)}, u32[]{:S(2)}) collective-permute-start(f32[3,32,4864]{2,1,0:T(8,128)} %collective-permute-done.top_ref), channel_id=1, source_target_pairs={{0,2},{2,4},{4,6},{6,8},{8,10},{10,12},{12,14},{14,16},{16,18},{18... | collective-permute-start | bytes 5603336 | tf_op jit(solution)/shard_map/ppermute | solution.py:24
  53.8 0.1 fusion.32
  53.9 0.1 dynamic-slice.3
  54.0 1.6 pad_dynamic-slice_fusion
  55.6 0.0 collective-permute-done.1.bottom_ref
  55.6 15.0 %shard_map.62 = (f32[3,32,4608]{2,1,0:T(8,128)S(1)}, f32[3,32,4608]{2,1,0:T(8,128)}) custom-call(f32[3,32,4864]{2,1,0:T(8,128)S(1)} %get-tuple-element.16.top_ref, f32[3,32,4864]{2,1,0:T(8,128)} %collective-permute-done.1.bottom_ref, f32[1,4864]{1,0:T(1,128)S(1)} %pad_dynamic-slice_fusion.3.modulus_ref, f32[1,4864]{1,0:T(1,128)S(1)} %copy-done), custom_call_target="tpu_custom_call" | custom-call | flops 112066560 | bytes 7471104 | tf_op jit(solution)/shard_map/pallas_call | solution.py:135
  70.6 1.3 collective-permute-start.3
  71.9 0.0 collective-permute-done.2.bottom_ref
  71.9 14.1 %shard_map.63 = (f32[3,32,4608]{2,1,0:T(8,128)S(1)}, f32[3,32,4608]{2,1,0:T(8,128)S(1)}) custom-call(f32[3,32,4864]{2,1,0:T(8,128)} %collective-permute-done.top_ref, f32[3,32,4864]{2,1,0:T(8,128)} %collective-permute-done.2.bottom_ref, f32[1,4864]{1,0:T(1,128)S(1)} %pad_dynamic-slice_fusion.3.modulus_ref, f32[1,4864]{1,0:T(1,128)S(1)} %copy-done), custom_call_target="tpu_custom_call" | custom-call | flops 112066560 | bytes 7471104 | tf_op jit(solution)/shard_map/pallas_call | solution.py:135
  86.0 1.5 collective-permute-start.4
  87.4 0.1 constant_dynamic-update-slice_fusion.1
  87.6 1.6 slice.32
  89.2 2.2 %slice.33 = f32[3,32,4608]{2,1,0:T(8,128)S(1)} slice(f32[3,32,4864]{2,1,0:T(8,128)} %collective-permute-done.1.bottom_ref), slice={[0:3], [0:32], [128:4736]} | slice | bytes 3538944 | tf_op jit(solution)/shard_map/slice | solution.py:297
  91.4 0.0 copy-done.8
  91.4 2.3 %fusion.24.mass_ref = f32[64,64]{1,0:T(8,128)} fusion(f32[4608]{0:T(1024)S(1)} %dynamic-slice.3, f32[3,32,4608]{2,1,0:T(8,128)S(1)} %slice.32, f32[3,32,4608]{2,1,0:T(8,128)S(1)} %pad_dynamic-slice_fusion), kind=kOutput, calls=%fused_computation.30 | convolution fusion | flops 342392832 | bytes 3573760 | tf_op jit(solution)/shard_map/ckn,cjn->kj/dot_general | solution.py:303
  93.7 1.6 slice.34
  95.3 0.1 constant_dynamic-update-slice_fusion
  95.4 0.0 copy-done.1
  95.4 0.0 copy-start.5
  95.5 1.7 fusion.18
  97.2 0.0 copy-done.3
  97.2 0.1 copy-done.5
  97.2 3.9 %fusion.27.stiff_ref = f32[64,64]{1,0:T(8,128)} fusion(f32[64,64]{1,0:T(8,128)S(1)} %fusion.18, f32[3,32,4608]{2,1,0:T(8,128)S(1)} %get-tuple-element.12, f32[3,32,4608]{2,1,0:T(8,128)} %get-tuple-element.11, f32[3,32,4608]{2,1,0:T(8,128)S(1)} %slice.34, f32[3,32,4608]{2,1,0:T(8,128)S(1)} %slice.33), kind=kOutput, calls=%fused_computation.33 | convolution fusion | flops 341512192 | bytes 7110656 | tf_op jit(solution)/shard_map/ckn,cjn->kj/dot_general | solution.py:303
  101.2 33.7 %shard_map.64 = (f32[64,64]{1,0:T(8,128)}, f32[64,64]{1,0:T(8,128)}, f32[64,64]{1,0:T(8,128)}) custom-call(f32[64,64]{1,0:T(8,128)} %fusion.27.stiff_ref, f32[64,64]{1,0:T(8,128)} %fusion.24.mass_ref), custom_call_target="tpu_custom_call" | custom-call | flops 10000000 | bytes 100000 | tf_op jit(solution)/shard_map/pallas_call | solution.py:245
  134.9 0.0 copy-start.6
  134.9 2.7 %fusion.1 = f32[32,3,4608]{2,0,1:T(8,128)S(1)} fusion(f32[4608]{0:T(1024)} %copy-done.8, f32[3,32,4608]{2,1,0:T(8,128)} %copy-done.3, f32[3,32,4608]{2,1,0:T(8,128)S(1)} %copy-done.2, f32[64,64]{1,0:T(8,128)} %get-tuple-element.14), kind=kOutput, calls=%fused_computation.3 | convolution fusion | flops 171638784 | bytes 5345280 | tf_op jit(solution)/shard_map/ckn,jk->jcn/dot_general | solution.py:313
  137.6 0.0 collective-permute-done.3
  137.6 0.0 collective-permute-done.4
  137.7 3.3 %convolution_subtract_fusion = f32[32,3,4608]{2,0,1:T(8,128)S(1)} fusion(f32[32,3,4608]{2,0,1:T(8,128)S(1)} %fusion.1, f32[3,64,4608]{2,1,0:T(8,128)S(1)} %copy-done.6, f32[3,32,4608]{2,1,0:T(8,128)} %collective-permute-done.4, f32[3,32,4608]{2,1,0:T(8,128)} %collective-permute-done.3, f32[64,64]{1,0:T(8,128)S(1)} %copy-done.11), kind=kOutput, calls=%fused_computation | convolution fusion | flops 172081152 | bytes 10633216 | tf_op jit(solution)/shard_map/ckn,jk->jcn/dot_general | solution.py:312
  141.0 0.5 collective-permute-start.5
  141.5 0.0 copy-done.9
  141.5 1.1 fusion.3
  142.6 3.1 %fusion = f32[32,3,1,4608]{3,0,1,2:T(8,128)S(1)} fusion(f32[32,3,4608]{2,0,1:T(8,128)S(1)} %fusion.3, f32[3,64,4608]{2,1,0:T(8,128)S(1)} %copy-done.6, f32[3,32,4608]{2,1,0:T(8,128)} %collective-permute-done.4, f32[3,32,4608]{2,1,0:T(8,128)} %collective-permute-done.3, f32[64,64]{1,0:T(8,128)S(1)} %copy-done.11), kind=kOutput, calls=%fused_computation.2 | convolution fusion | flops 172081152 | bytes 10633216 | tf_op jit(solution)/shard_map/ckn,jk->jcn/dot_general | solution.py:312
  145.7 2.0 %broadcast_in_dim.23 = f32[32,3,1,9216]{3,2,1,0:T(1,128)S(1)} broadcast(f32[]{:T(128)} %constant.10.clone.1), dimensions={} | broadcast | bytes 3538948 | tf_op jit(solution)/shard_map/broadcast_in_dim | solution.py:320
  147.7 0.0 copy-start.13
  147.8 2.0 %copy_dynamic-update-slice_fusion.1 = f32[32,3,1,9216]{3,2,1,0:T(1,128)S(1)} fusion(f32[32,3,1,9216]{3,2,1,0:T(1,128)S(1)} %broadcast_in_dim.23, s32[]{:T(128)S(6)} %select_n.35, f32[32,3,1,4608]{3,0,1,2:T(8,128)S(1)} %fusion), kind=kLoop, calls=%fused_computation.23 | loop fusion | bytes 3538948 | tf_op jit(solution)/shard_map/dynamic_update_slice | solution.py:319
  149.7 26.7 %collective-permute-done.5 = f32[32,3,4608]{2,0,1:T(8,128)S(1)} collective-permute-done((f32[32,3,4608]{2,0,1:T(8,128)S(1)}, f32[32,3,4608]{2,0,1:T(8,128)S(1)}, u32[]{:S(2)}, u32[]{:S(2)}) %collective-permute-start.5) | collective-permute-done | bytes 1769504 | tf_op jit(solution)/shard_map/ppermute | solution.py:263
  176.4 1.9 %copy_dynamic-update-slice_fusion = f32[32,3,1,9216]{3,2,1,0:T(1,128)S(1)} fusion(f32[32,3,1,9216]{3,2,1,0:T(1,128)S(1)} %copy_dynamic-update-slice_fusion.1, s32[]{:T(128)S(6)} %select_n.36, f32[32,3,1,4608]{3,0,1,2:T(8,128)S(1)} %bitcast.33), kind=kLoop, calls=%fused_computation.22 | loop fusion | bytes 3538948 | tf_op jit(solution)/shard_map/dynamic_update_slice | solution.py:319
  178.3 0.0 copy-start.7
  178.3 0.7 copy.20
  179.0 1.1 copy-done.7
  (20 shorter events, 0.0 us)
Async XLA Ops:
  5.0 8.0 %copy-start.10 = (s32[1,9216]{1,0:T(1,128)S(1)}, s32[1,9216]{1,0:T(1,128)}, u32[]{:S(2)}) copy-start(s32[1,9216]{1,0:T(1,128)} %param.5) | copy-start | bytes 110596
  5.1 8.0 %copy-start.14 = (f32[16]{0:T(128)S(1)}, f32[16]{0:T(128)}, u32[]{:S(2)}) copy-start(f32[16]{0:T(128)} %param.6) | copy-start | bytes 196
  7.3 48.3 %copy-start = (f32[1,4864]{1,0:T(1,128)S(1)}, f32[1,4864]{1,0:T(1,128)}, u32[]{:S(2)}) copy-start(f32[1,4864]{1,0:T(1,128)} %constant.31.clone.inside_ref) | copy-start | bytes 58372
  7.4 43.9 %collective-permute-start = (f32[3,32,4864]{2,1,0:T(8,128)S(1)}, f32[3,32,4864]{2,1,0:T(8,128)}, u32[]{:S(2)}, u32[]{:S(2)}) collective-permute-start(f32[3,32,4864]{2,1,0:T(8,128)S(1)} %get-tuple-element.17), channel_id=1, source_target_pairs={{0,1},{1,0},{2,3},{3,2},{4,5},{5,4},{6,7},{7,6},{8,9},{9,8},{10,11... | collective-permute-start | bytes 5603336 | tf_op jit(solution)/shard_map/ppermute | solution.py:263
  10.4 45.2 %collective-permute-start.1 = (f32[3,32,4864]{2,1,0:T(8,128)S(1)}, f32[3,32,4864]{2,1,0:T(8,128)}, u32[]{:S(2)}, u32[]{:S(2)}) collective-permute-start(f32[3,32,4864]{2,1,0:T(8,128)S(1)} %get-tuple-element.16.top_ref), channel_id=1, source_target_pairs={{0,2},{2,4},{4,6},{6,8},{8,10},{10,12},{12,14},{14,16},{16,18},{18... | collective-permute-start | bytes 5603336 | tf_op jit(solution)/shard_map/ppermute | solution.py:24
  51.2 20.7 %collective-permute-start.2 = (f32[3,32,4864]{2,1,0:T(8,128)}, f32[3,32,4864]{2,1,0:T(8,128)}, u32[]{:S(2)}, u32[]{:S(2)}) collective-permute-start(f32[3,32,4864]{2,1,0:T(8,128)} %collective-permute-done.top_ref), channel_id=1, source_target_pairs={{0,2},{2,4},{4,6},{6,8},{8,10},{10,12},{12,14},{14,16},{16,18},{18... | collective-permute-start | bytes 5603336 | tf_op jit(solution)/shard_map/ppermute | solution.py:24
  53.9 37.5 %copy-start.8 = (f32[4608]{0:T(1024)}, f32[4608]{0:T(1024)S(1)}, u32[]{:S(2)}) copy-start(f32[4608]{0:T(1024)S(1)} %dynamic-slice.3) | copy-start | bytes 55300
  55.6 39.9 %copy-start.1 = (f32[3,32,4608]{2,1,0:T(8,128)}, f32[3,32,4608]{2,1,0:T(8,128)S(1)}, u32[]{:S(2)}) copy-start(f32[3,32,4608]{2,1,0:T(8,128)S(1)} %pad_dynamic-slice_fusion) | copy-start | bytes 5308420
  70.6 67.0 %collective-permute-start.3 = (f32[3,32,4608]{2,1,0:T(8,128)}, f32[3,32,4608]{2,1,0:T(8,128)}, u32[]{:S(2)}, u32[]{:S(2)}) collective-permute-start(f32[3,32,4608]{2,1,0:T(8,128)} %get-tuple-element.11), channel_id=1, source_target_pairs={{2,0},{4,2},{6,4},{8,6},{10,8},{12,10},{14,12},{16,14},{18,16},{20... | collective-permute-start | bytes 5308424 | tf_op jit(solution)/shard_map/ppermute | solution.py:24
  86.0 51.7 %collective-permute-start.4 = (f32[3,32,4608]{2,1,0:T(8,128)S(1)}, f32[3,32,4608]{2,1,0:T(8,128)}, u32[]{:S(2)}, u32[]{:S(2)}) collective-permute-start(f32[3,32,4608]{2,1,0:T(8,128)S(1)} %get-tuple-element.12), channel_id=1, source_target_pairs={{2,0},{4,2},{6,4},{8,6},{10,8},{12,10},{14,12},{16,14},{18,16},{20... | collective-permute-start | bytes 5308424 | tf_op jit(solution)/shard_map/ppermute | solution.py:24
  89.2 8.0 %copy-start.3 = (f32[3,32,4608]{2,1,0:T(8,128)}, f32[3,32,4608]{2,1,0:T(8,128)S(1)}, u32[]{:S(2)}) copy-start(f32[3,32,4608]{2,1,0:T(8,128)S(1)} %slice.32) | copy-start | bytes 5308420
  95.4 1.8 copy-start.5
  97.2 37.7 %copy-start.2 = (f32[3,32,4608]{2,1,0:T(8,128)S(1)}, f32[3,32,4608]{2,1,0:T(8,128)}, u32[]{:S(2)}) copy-start(f32[3,32,4608]{2,1,0:T(8,128)} %copy-done.1) | copy-start | bytes 5308420
  134.9 2.8 %copy-start.6 = (f32[3,64,4608]{2,1,0:T(8,128)S(1)}, f32[3,64,4608]{2,1,0:T(8,128)}, u32[]{:S(2)}) copy-start(f32[3,64,4608]{2,1,0:T(8,128)} %copy-done.5) | copy-start | bytes 10616836
  134.9 2.8 %copy-start.11 = (f32[64,64]{1,0:T(8,128)S(1)}, f32[64,64]{1,0:T(8,128)}, u32[]{:S(2)}) copy-start(f32[64,64]{1,0:T(8,128)} %get-tuple-element.13) | copy-start | bytes 49156
  137.7 3.8 %copy-start.4 = (f32[3,32,4608]{2,1,0:T(8,128)S(1)}, f32[3,32,4608]{2,1,0:T(8,128)}, u32[]{:S(2)}) copy-start(f32[3,32,4608]{2,1,0:T(8,128)} %copy-done.3) | copy-start | bytes 5308420
  137.7 3.8 %copy-start.9 = (f32[4608]{0:T(1024)S(1)}, f32[4608]{0:T(1024)}, u32[]{:S(2)}) copy-start(f32[4608]{0:T(1024)} %copy-done.8) | copy-start | bytes 55300
  137.7 3.8 %copy-start.12 = (f32[64,64]{1,0:T(8,128)S(1)}, f32[64,64]{1,0:T(8,128)}, u32[]{:S(2)}) copy-start(f32[64,64]{1,0:T(8,128)} %get-tuple-element.14) | copy-start | bytes 49156
  141.0 35.4 %collective-permute-start.5 = (f32[32,3,4608]{2,0,1:T(8,128)S(1)}, f32[32,3,4608]{2,0,1:T(8,128)S(1)}, u32[]{:S(2)}, u32[]{:S(2)}) collective-permute-start(f32[32,3,4608]{2,0,1:T(8,128)S(1)} %convolution_subtract_fusion), channel_id=1, source_target_pairs={{0,1},{1,0},{2,3},{3,2},{4,5},{5,4},{6,7},{7,6},{8,9},{9,8},{10,11... | collective-permute-start | bytes 5308424 | tf_op jit(solution)/shard_map/ppermute | solution.py:263
  147.7 30.6 %copy-start.13 = (f32[64,64]{1,0:T(8,128)S(1)}, f32[64,64]{1,0:T(8,128)}, u32[]{:S(2)}) copy-start(f32[64,64]{1,0:T(8,128)} %get-tuple-element.21) | copy-start | bytes 49156
  178.3 1.8 %copy-start.7 = (f32[32,3,1,9216]{3,2,1,0:T(1,128)}, f32[32,3,1,9216]{3,2,1,0:T(1,128)S(1)}, u32[]{:S(2)}) copy-start(f32[32,3,1,9216]{3,2,1,0:T(1,128)S(1)} %copy_dynamic-update-slice_fusion) | copy-start | bytes 10616836

commit v3 on v2

--- a/solution.py
+++ b/solution.py
@@ -139,13 +139,13 @@
         out_specs=[out_block, out_block],
         out_shape=[shape, shape],
         cost_estimate=pl.CostEstimate(
-            flops=240 * top.size, bytes_accessed=16 * top.size, transcendentals=0
+            flops=36000 * top.size, bytes_accessed=16 * top.size, transcendentals=0
         ),
         compiler_params=pltpu.CompilerParams(vmem_limit_bytes=32 * 2**20),
     )(top, bottom, modulus, inside)
 
 
-CHUNKS = (2304, 1152, 384, 128)
+CHUNKS = (4608, 2304, 1152, 384, 128)
 
 
 def densities(classes, level_density):
@@ -153,6 +153,66 @@
     level_index = lax.iota(jnp.int32, levels).reshape(levels, 1, 1)
     matches = classes[None] == level_index
     return jnp.sum(jnp.where(matches, level_density[:, None, None], 0.0), 0)
+
+
+def split(x):
+    upper = x.astype(jnp.bfloat16)
+    lower = (x - upper.astype(jnp.float32)).astype(jnp.bfloat16)
+    return jnp.concatenate([upper, lower], 0)
+
+
+def gram_kernel(block_count, lanes_own, *refs):
+    density_ref, stiff_ref, mass_ref = refs[4 * block_count :]
+
+    def gathered(which, start):
+        parts = refs[which * block_count : (which + 1) * block_count]
+        return jnp.concatenate([ref[0, :, start : start + lanes_own] for ref in parts], 0)
+
+    def product(a, b):
+        return lax.dot_general(
+            a, b, (((1,), (1,)), ((), ())), preferred_element_type=jnp.float32
+        )
+
+    def folded(wide):
+        size = wide.shape[0] // 2
+        return wide[:size, :size] + (wide[size:, :size] + wide[:size, size:])
+
+    top = gathered(0, MARGIN)
+    size = top.shape[0]
+    right = [split(gathered(2, 0)), split(top * density_ref[...])]
+    both = product(split(top), jnp.concatenate(right, 0))
+    low = product(split(gathered(1, MARGIN)), split(gathered(3, 0)))
+    stiff = folded(both[:, : 2 * size]) + folded(low)
+    mass = folded(both[:, 2 * size :])
+
+    @pl.when(pl.program_id(0) == 0)
+    def first():
+        stiff_ref[...] = stiff
+        mass_ref[...] = mass
+
+    @pl.when(pl.program_id(0) > 0)
+    def later():
+        stiff_ref[...] += stiff
+        mass_ref[...] += mass
+
+
+def grams(tops, bottoms, force_tops, force_bottoms, density):
+    arrays = tops + bottoms + force_tops + force_bottoms
+    size = sum(top.shape[1] for top in tops)
+    shape = jax.ShapeDtypeStruct((size, size), jnp.float32)
+    out_block = pl.BlockSpec((size, size), lambda c: (0, 0))
+    return pl.pallas_call(
+        functools.partial(gram_kernel, len(tops), density.shape[1]),
+        grid=(tops[0].shape[0],),
+        in_specs=[pl.BlockSpec((1,) + x.shape[1:], lambda c: (c, 0, 0)) for x in arrays]
+        + [pl.BlockSpec(density.shape, lambda c: (0, 0))],
+        out_specs=[out_block, out_block],
+        out_shape=[shape, shape],
+        cost_estimate=pl.CostEstimate(
+            flops=5 * 10**9, bytes_accessed=10**7, transcendentals=0
+        ),
+        compiler_params=pltpu.CompilerParams(vmem_limit_bytes=48 * 2**20),
+    )(*arrays, density)
 
 
 def dot(a, b, contract):
@@ -280,43 +340,46 @@
 
     vectors = jnp.transpose(subspace[:, :, 0], (1, 0, 2))
     padded = jnp.pad(vectors, ((0, 0), (0, 0), (MARGIN, MARGIN)))
-    tops, forces, bottoms = [], [], []
+    pieces = 2 if mode_count % 16 == 0 else 1
+    rows = mode_count // pieces
+    tops = []
     for s in range(groups):
         target = lax.rem(group + s, groups)
-        window = lax.dynamic_slice(
-            padded, (0, 0, target * lanes_own), (comps, mode_count, wide)
-        )
-        top = window if s == 0 else rotated(window, "modes", s)
-        tops.append(top)
+        for piece in range(1 if s == 0 else pieces):
+            size = mode_count if s == 0 else rows
+            window = lax.dynamic_slice(
+                padded, (0, piece * rows, target * lanes_own), (comps, size, wide)
+            )
+            tops.append(window if s == 0 else rotated(window, "modes", s))
+    bottoms, force_tops, force_bottoms = [], [], []
+    for index, top in enumerate(tops):
+        if index >= 2:
+            top, force_bottoms[0] = lax.optimization_barrier((top, force_bottoms[0]))
+            tops[index] = top
         bottoms.append(shifted(top, "mesh", 1))
-    for top, bottom in zip(tops, bottoms):
-        forces.append(layer_forces(top, bottom, modulus, inside))
-    returned = [shifted(force[1], "mesh", -1) for force in forces]
+        force_top, force_bottom = layer_forces(top, bottoms[-1], modulus, inside)
+        force_tops.append(force_top)
+        force_bottoms.append(force_bottom)
+    returned = [shifted(force, "mesh", -1) for force in force_bottoms]
+    part_stiff, part_mass = grams(tops, bottoms, force_tops, force_bottoms, density)
+    ritz_matrix, rotate, mixed_rotate = ritz_solve(part_stiff, part_mass, mode_count, total_dofs)
     middle = slice(MARGIN, MARGIN + lanes_own)
-    top = jnp.concatenate([t[:, :, middle] for t in tops], 1)
-    bottom = jnp.concatenate([b[:, :, middle] for b in bottoms], 1)
-    force_top = jnp.concatenate([f[0] for f in forces], 1)
-    force_bottom = jnp.concatenate([f[1] for f in forces], 1)
-    mass = top * density
-
-    def gram(a, b):
-        return jnp.einsum("ckn,cjn->kj", a, b, precision=high)
-
-    part_stiff = gram(top, force_top) + gram(bottom, force_bottom)
-    part_mass = gram(top, mass)
-    ritz_matrix, rotate, mixed_rotate = ritz_solve(part_stiff, part_mass, mode_count, total_dofs)
-    image = force_top + jnp.concatenate(returned, 1)
+    mass = jnp.concatenate([t[:, :, middle] for t in tops], 1) * density
+    image = jnp.concatenate([f + r for f, r in zip(force_tops, returned)], 1)
     parts = []
     for s in reversed(range(groups)):
-        columns = slice(s * mode_count, (s + 1) * mode_count)
-        part = jnp.einsum("ckn,jk->jcn", image, rotate[columns], precision=high)
-        part = part - jnp.einsum("ckn,jk->jcn", mass, mixed_rotate[columns], precision=high)
-        parts.append(part if s == 0 else rotated(part, "modes", -s))
+        for piece in range(1 if s == 0 else pieces):
+            size = mode_count if s == 0 else rows
+            start = s * mode_count + piece * rows
+            columns = slice(start, start + size)
+            part = jnp.einsum("ckn,jk->jcn", image, rotate[columns], precision=high)
+            part = part - jnp.einsum("ckn,jk->jcn", mass, mixed_rotate[columns], precision=high)
+            parts.append((s, piece * rows, part if s == 0 else rotated(part, "modes", -s)))
     parts = parts[::-1]
     residual = jnp.zeros((mode_count, comps, nodes), jnp.float32)
-    for s, part in enumerate(parts):
+    for s, start, part in parts:
         source = lax.rem(group + s, groups)
-        residual = lax.dynamic_update_slice(residual, part, (0, 0, source * lanes_own))
+        residual = lax.dynamic_update_slice(residual, part, (start, 0, source * lanes_own))
     return (residual[:, :, None], ritz_matrix)
 
 

time: 181 us -> 194 us (1.072)
  matrix products: 18.1 us -> 10.4 us
  starting transfers between devices: 11.5 us -> 17.4 us
  other arithmetic: 0.25 us -> 5.47 us
  Pallas kernels: 62.8 us -> 66.8 us
  waiting for transfers between devices: 64.6 us -> 67.3 us
  local copies, waits for them, and re-layouts: 21.9 us -> 24.4 us
    dot_general x3 -> x0, matrix products: 7.91 us -> none  [gram(): return jnp.einsum('ckn,cjn->kj', a, b, precision=high)]
    pallas_call x0 -> x1, Pallas kernels: none -> 6.79 us  [grams(): pl.pallas_call(functools.partial(gram_kernel, len(tops), density.shape[1]...]
    add x0 -> x3, other arithmetic: none -> 5.22 us  [per_device(): image = jnp.concatenate([f + r for f, r in zip(force_tops, returned)], 1)]
    pallas_call x2 -> x3, Pallas kernels: 29 us -> 23.9 us  [layer_forces(): pl.pallas_call(functools.partial(layer_kernel, chunk, lanes_own), grid=(m...]
    ppermute x4 -> x6, starting transfers between devices: 8 us -> 12.9 us  [shifted(): return lax.ppermute(x, axis, pairs)]
    dot_general x2 -> x3, matrix products: 3.75 us -> 6.72 us  [per_device(): jnp.einsum('ckn,jk->jcn', mass, mixed_rotate[columns], precision=high)]
    dot_general x2 -> x3, matrix products: 6.4 us -> 3.66 us  [per_device(): part = jnp.einsum('ckn,jk->jcn', image, rotate[columns], precision=high)]
    ppermute x2 -> x4, waiting for transfers between devices: 64.6 us -> 67.3 us  [rotated(): return lax.ppermute(x, axis, [(i, (i + by) % size) for i in range(size)])]
  transfers between devices with their start and end apart: 6 -> 10, of which waited for: 2 -> 2; matrix products, arithmetic and copies ran while one was open for 15% -> 14% of each run, Pallas kernels for 35% -> 35%
where the time goes in v3:
time: 194 us; the launch traced here: 193 us
  waiting for transfers between devices  67.3 us (35%)
  Pallas kernels  66.8 us (34%)
  local copies, waits for them, and re-layouts  24.4 us (13%)
  starting transfers between devices  17.4 us (9%)
  matrix products  10.4 us (5%)
  other arithmetic  5.47 us (3%)
    ppermute x4, waiting for transfers between devices, rotated(): return lax.ppermute(x, axis, [(i, (i + by) % size) for i in range(size)])  67.3 us
    pallas_call x1, Pallas kernels, ritz_solve(): pl.pallas_call(functools.partial(ritz_kernel, axes, mode_count, total_dof...  36.2 us
    pallas_call x3, Pallas kernels, layer_forces(): pl.pallas_call(functools.partial(layer_kernel, chunk, lanes_own), grid=(m...  23.9 us
    ppermute x6, starting transfers between devices, shifted(): return lax.ppermute(x, axis, pairs)  12.9 us
    unnamed x40, local copies, waits for them, and re-layouts  7.85 us
    pallas_call x1, Pallas kernels, grams(): pl.pallas_call(functools.partial(gram_kernel, len(tops), density.shape[1]...  6.79 us
    dot_general x3, matrix products, per_device(): jnp.einsum('ckn,jk->jcn', mass, mixed_rotate[columns], precision=high)  6.72 us
    slice x3, local copies, waits for them, and re-layouts, per_device(): mass = jnp.concatenate([t[:, :, middle] for t in tops], 1) * density  5.93 us
  transfers between devices with their start and end apart: 10, of which 2 were waited for; matrix products, arithmetic and copies ran while one was open for 14% of the time, Pallas kernels for 35%

profile of v3, /device:TPU:0, one launch (start us, length us, event | category | flops | bytes accessed | tf_op | source)
XLA Modules:
  0.0 192.8 jit_solution(3494120252106614390)
XLA Ops:
  0.6 4.4 %copy.18 = f32[32,3,1,9216]{3,0,1,2:T(8,128)} copy(f32[32,3,1,9216]{3,2,1,0:T(1,128)} %param.4) | data formatting | bytes 7077888 | tf_op args[0]
  5.0 1.6 pad_dynamic-slice_fusion.3.top_ref.refs_0_
  6.7 0.0 copy-start.14
  6.7 0.0 copy-start.18
  6.7 0.0 copy-start.8
  6.7 3.7 %collective-permute-start.2 = (f32[3,32,4864]{2,1,0:T(8,128)S(1)}, f32[3,32,4864]{2,1,0:T(8,128)}, u32[]{:S(2)}, u32[]{:S(2)}) collective-permute-start(f32[3,32,4864]{2,1,0:T(8,128)S(1)} %pad_dynamic-slice_fusion.3.top_ref.refs_0_), channel_id=1, source_target_pairs={{0,2},{2,4},{4,6},{6,8},{8,10},{10,12},{12,14},{14,16},{16,18},{18... | collective-permute-start | bytes 5603336 | tf_op jit(solution)/shard_map/ppermute | solution.py:24
  10.4 2.9 %pad_dynamic-slice_fusion.2 = (f32[3,16,4864]{2,1,0:T(8,128)}, f32[3,16,4864]{2,1,0:T(8,128)}) fusion(s32[]{:T(128)S(6)} %select_n.33, f32[3,32,9216]{2,1,0:T(8,128)} %bitcast.30), kind=kLoop, calls=%fused_computation.9 | loop fusion | bytes 5406724 | tf_op jit(solution)/shard_map/dynamic_slice | solution.py:350
  13.3 2.4 %collective-permute-start.1 = (f32[3,16,4864]{2,1,0:T(8,128)}, f32[3,16,4864]{2,1,0:T(8,128)S(1)}, u32[]{:S(2)}, u32[]{:S(2)}) collective-permute-start(f32[3,16,4864]{2,1,0:T(8,128)} %get-tuple-element.29), channel_id=1, source_target_pairs={{0,1},{1,0},{2,3},{3,2},{4,5},{5,4},{6,7},{7,6},{8,9},{9,8},{10,11... | collective-permute-start | bytes 2801672 | tf_op jit(solution)/shard_map/ppermute | solution.py:323
  15.7 0.0 collective-permute-start
  15.7 0.2 select_reduce_fusion
  15.9 0.1 fusion.4
  16.0 41.5 %collective-permute-done.top_ref.refs_1_ = f32[3,16,4864]{2,1,0:T(8,128)} collective-permute-done((f32[3,16,4864]{2,1,0:T(8,128)}, f32[3,16,4864]{2,1,0:T(8,128)}, u32[]{:S(2)}, u32[]{:S(2)}) %collective-permute-start) | collective-permute-done | bytes 933920 | tf_op jit(solution)/shard_map/ppermute | solution.py:323
  57.5 2.1 %collective-permute-start.3 = (f32[3,16,4864]{2,1,0:T(8,128)}, f32[3,16,4864]{2,1,0:T(8,128)S(1)}, u32[]{:S(2)}, u32[]{:S(2)}) collective-permute-start(f32[3,16,4864]{2,1,0:T(8,128)} %collective-permute-done.top_ref.refs_1_), channel_id=1, source_target_pairs={{0,2},{2,4},{4,6},{6,8},{8,10},{10,12},{12,14},{14,16},{16,18},{18... | collective-permute-start | bytes 2801672 | tf_op jit(solution)/shard_map/ppermute | solution.py:24
  59.6 11.3 %shard_map.62 = (f32[3,32,4608]{2,1,0:T(8,128)S(1)}, f32[3,32,4608]{2,1,0:T(8,128)}) custom-call(f32[3,32,4864]{2,1,0:T(8,128)S(1)} %pad_dynamic-slice_fusion.3.top_ref.refs_0_, f32[3,32,4864]{2,1,0:T(8,128)} %collective-permute-done.2.bottom_ref.refs_3_, f32[1,4864]{1,0:T(1,128)S(1)} %pad_dynamic-slice_fusion.4.modulus_ref, f32[1,4864]{1,0:T(1,128)S(1)} %copy-done.8), custom_call_target="tpu_custom_call" | custom-call | flops 16809984000 | bytes 7471104 | tf_op jit(solution)/shard_map/pallas_call | solution.py:135
  70.8 3.2 %collective-permute-start.4 = (f32[3,16,4864]{2,1,0:T(8,128)S(1)}, f32[3,16,4864]{2,1,0:T(8,128)}, u32[]{:S(2)}, u32[]{:S(2)}) collective-permute-start(f32[3,16,4864]{2,1,0:T(8,128)S(1)} %collective-permute-done.1.top_ref.refs_2_), channel_id=1, source_target_pairs={{0,2},{2,4},{4,6},{6,8},{8,10},{10,12},{12,14},{14,16},{16,18},{18... | collective-permute-start | bytes 2801672 | tf_op jit(solution)/shard_map/ppermute | solution.py:24
  74.1 6.1 %shard_map.63 = (f32[3,16,4608]{2,1,0:T(8,128)S(1)}, f32[3,16,4608]{2,1,0:T(8,128)S(1)}) custom-call(f32[3,16,4864]{2,1,0:T(8,128)} %collective-permute-done.top_ref.refs_1_, f32[3,16,4864]{2,1,0:T(8,128)S(1)} %collective-permute-done.3.bottom_ref.refs_4_, f32[1,4864]{1,0:T(1,128)S(1)} %pad_dynamic-slice_fusion.4.modulus_ref, f32[1,4864]{1,0:T(1,128)S(1)} %copy-done.8), custom_call_target="tpu_custom_call" | custom-call | flops 8404992000 | bytes 3735552 | tf_op jit(solution)/shard_map/pallas_call | solution.py:135
  80.2 1.3 collective-permute-start.6
  81.5 0.1 dynamic-slice.3
  81.6 2.8 %pad_dynamic-slice_fusion = f32[3,32,4608]{2,1,0:T(8,128)} fusion(s32[]{:T(128)S(6)} %add.64, f32[3,32,9216]{2,1,0:T(8,128)} %bitcast.31), kind=kLoop, calls=%fused_computation.7 | loop fusion | bytes 5308420 | tf_op jit(solution)/shard_map/slice | solution.py:367
  84.4 2.1 %slice.36 = f32[3,16,4608]{2,1,0:T(8,128)} slice(f32[3,16,4864]{2,1,0:T(8,128)} %collective-permute-done.top_ref.refs_1_), slice={[0:3], [0:16], [128:4736]} | slice | bytes 1769472 | tf_op jit(solution)/shard_map/slice | solution.py:367
  86.6 1.0 slice.31
  87.5 1.3 collective-permute-start.5
  88.8 2.2 %add.60 = f32[3,16,4608]{2,1,0:T(8,128)} add(f32[3,16,4608]{2,1,0:T(8,128)S(1)} %get-tuple-element.18.refs_7_, f32[3,16,4608]{2,1,0:T(8,128)} %collective-permute-done.6) | non-fusion elementwise | flops 221184 | bytes 2654208 | tf_op jit(solution)/shard_map/add | solution.py:368
  91.1 6.6 %shard_map.64 = (f32[3,16,4608]{2,1,0:T(8,128)S(1)}, f32[3,16,4608]{2,1,0:T(8,128)}) custom-call(f32[3,16,4864]{2,1,0:T(8,128)S(1)} %collective-permute-done.1.top_ref.refs_2_, f32[3,16,4864]{2,1,0:T(8,128)} %collective-permute-done.4.bottom_ref.refs_5_, f32[1,4864]{1,0:T(1,128)S(1)} %pad_dynamic-slice_fusion.4.modulus_ref, f32[1,4864]{1,0:T(1,128)S(1)} %copy-done.8), custom_call_target="tpu_custom_call" | custom-call | flops 8404992000 | bytes 3735552 | tf_op jit(solution)/shard_map/pallas_call | solution.py:135
  97.6 1.3 collective-permute-start.7
  98.9 6.8 %shard_map.65 = (f32[64,64]{1,0:T(8,128)S(1)}, f32[64,64]{1,0:T(8,128)S(1)}) custom-call(f32[3,32,4864]{2,1,0:T(8,128)} %copy-done, f32[3,16,4864]{2,1,0:T(8,128)} %collective-permute-done.top_ref.refs_1_, f32[3,16,4864]{2,1,0:T(8,128)S(1)} %collective-permute-done.1.top_ref.refs_2_, f32[3,32,4864]{2,1,0:T(8,128)} %collective-permute-done.2.bottom_ref.refs_3_, ...), custom_call_target="tpu_custom_call" | custom-call | flops 5000000000 | bytes 10000000 | tf_op jit(solution)/shard_map/pallas_call | solution.py:204
  105.7 0.0 copy-start.3
  105.7 0.6 copy-done.3
  106.4 0.6 copy-done.4
  107.0 36.2 %shard_map.66 = (f32[64,64]{1,0:T(8,128)}, f32[64,64]{1,0:T(8,128)}, f32[64,64]{1,0:T(8,128)}) custom-call(f32[64,64]{1,0:T(8,128)} %copy-done.3, f32[64,64]{1,0:T(8,128)} %copy-done.4), custom_call_target="tpu_custom_call" | custom-call | flops 10000000 | bytes 100000 | tf_op jit(solution)/shard_map/pallas_call | solution.py:305
  143.1 3.0 %fusion.1 = f32[16,3,4608]{2,0,1:T(8,128)S(1)} fusion(f32[3,16,4608]{2,1,0:T(8,128)} %slice.31, f32[3,16,4608]{2,1,0:T(8,128)} %slice.36, f32[3,32,4608]{2,1,0:T(8,128)} %pad_dynamic-slice_fusion, f32[4608]{0:T(1024)S(1)} %dynamic-slice.3, f32[64,64]{1,0:T(8,128)} %get-tuple-element.26), kind=kOutput, calls=%fused_computation.12 | convolution fusion | flops 87588864 | bytes 4450304 | tf_op jit(solution)/shard_map/ckn,jk->jcn/dot_general | solution.py:376
  146.2 2.6 %fusion.2 = f32[16,3,4608]{2,0,1:T(8,128)S(1)} fusion(f32[3,16,4608]{2,1,0:T(8,128)} %slice.31, f32[3,16,4608]{2,1,0:T(8,128)} %slice.36, f32[3,32,4608]{2,1,0:T(8,128)S(1)} %copy-done.10, f32[4608]{0:T(1024)S(1)} %dynamic-slice.3, f32[64,64]{1,0:T(8,128)S(1)} %copy-done.17), kind=kOutput, calls=%fused_computation.13 | convolution fusion | flops 87588864 | bytes 4452352 | tf_op jit(solution)/shard_map/ckn,jk->jcn/dot_general | solution.py:376
  148.9 1.1 fusion.3
  150.0 0.4 copy-done.2
  150.3 1.7 add.59
  152.0 1.3 add.61
  153.4 1.2 convolution_subtract_fusion.1
  154.5 0.6 collective-permute-start.9
  155.1 1.2 convolution_subtract_fusion.2
  156.3 1.6 collective-permute-start.8
  157.9 1.3 fusion
  159.2 1.8 broadcast_in_dim.25
  161.0 2.2 %copy_dynamic-update-slice_fusion = f32[32,3,1,9216]{3,2,1,0:T(1,128)S(1)} fusion(f32[32,3,1,9216]{3,2,1,0:T(1,128)S(1)} %broadcast_in_dim.25, s32[]{:T(128)S(6)} %select_n.37, f32[32,3,1,4608]{3,0,1,2:T(8,128)S(1)} %fusion), kind=kLoop, calls=%fused_computation.11 | loop fusion | bytes 3538948 | tf_op jit(solution)/shard_map/dynamic_update_slice | solution.py:382
  163.2 25.8 %collective-permute-done.8 = f32[16,3,4608]{2,0,1:T(8,128)S(1)} collective-permute-done((f32[16,3,4608]{2,0,1:T(8,128)S(1)}, f32[16,3,4608]{2,0,1:T(8,128)S(1)}, u32[]{:S(2)}, u32[]{:S(2)}) %collective-permute-start.8) | collective-permute-done | bytes 884768 | tf_op jit(solution)/shard_map/ppermute | solution.py:323
  189.1 1.0 copy_dynamic-update-slice_fusion.2
  190.0 1.0 copy_dynamic-update-slice_fusion.1
  191.0 0.7 copy.23
  191.7 1.1 copy-done.11
  (40 shorter events, 0.1 us)
Async XLA Ops:
  6.7 64.2 %copy-start = (f32[3,32,4864]{2,1,0:T(8,128)}, f32[3,32,4864]{2,1,0:T(8,128)S(1)}, u32[]{:S(2)}) copy-start(f32[3,32,4864]{2,1,0:T(8,128)S(1)} %pad_dynamic-slice_fusion.3.top_ref.refs_0_) | copy-start | bytes 5603332
  6.7 9.1 %copy-start.14 = (s32[1,9216]{1,0:T(1,128)S(1)}, s32[1,9216]{1,0:T(1,128)}, u32[]{:S(2)}) copy-start(s32[1,9216]{1,0:T(1,128)} %param.5) | copy-start | bytes 110596
  6.7 9.0 %copy-start.18 = (f32[16]{0:T(128)S(1)}, f32[16]{0:T(128)}, u32[]{:S(2)}) copy-start(f32[16]{0:T(128)} %param.6) | copy-start | bytes 196
  6.7 52.9 %copy-start.8 = (f32[1,4864]{1,0:T(1,128)S(1)}, f32[1,4864]{1,0:T(1,128)}, u32[]{:S(2)}) copy-start(f32[1,4864]{1,0:T(1,128)} %constant.34.clone.inside_ref) | copy-start | bytes 58372
  6.7 52.8 %collective-permute-start.2 = (f32[3,32,4864]{2,1,0:T(8,128)S(1)}, f32[3,32,4864]{2,1,0:T(8,128)}, u32[]{:S(2)}, u32[]{:S(2)}) collective-permute-start(f32[3,32,4864]{2,1,0:T(8,128)S(1)} %pad_dynamic-slice_fusion.3.top_ref.refs_0_), channel_id=1, source_target_pairs={{0,2},{2,4},{4,6},{6,8},{8,10},{10,12},{12,14},{14,16},{16,18},{18... | collective-permute-start | bytes 5603336 | tf_op jit(solution)/shard_map/ppermute | solution.py:24
  13.3 57.5 %collective-permute-start.1 = (f32[3,16,4864]{2,1,0:T(8,128)}, f32[3,16,4864]{2,1,0:T(8,128)S(1)}, u32[]{:S(2)}, u32[]{:S(2)}) collective-permute-start(f32[3,16,4864]{2,1,0:T(8,128)} %get-tuple-element.29), channel_id=1, source_target_pairs={{0,1},{1,0},{2,3},{3,2},{4,5},{5,4},{6,7},{7,6},{8,9},{9,8},{10,11... | collective-permute-start | bytes 2801672 | tf_op jit(solution)/shard_map/ppermute | solution.py:323
  15.7 41.8 %collective-permute-start = (f32[3,16,4864]{2,1,0:T(8,128)}, f32[3,16,4864]{2,1,0:T(8,128)}, u32[]{:S(2)}, u32[]{:S(2)}) collective-permute-start(f32[3,16,4864]{2,1,0:T(8,128)} %get-tuple-element.28), channel_id=1, source_target_pairs={{0,1},{1,0},{2,3},{3,2},{4,5},{5,4},{6,7},{7,6},{8,9},{9,8},{10,11... | collective-permute-start | bytes 2801672 | tf_op jit(solution)/shard_map/ppermute | solution.py:323
  57.5 16.6 %collective-permute-start.3 = (f32[3,16,4864]{2,1,0:T(8,128)}, f32[3,16,4864]{2,1,0:T(8,128)S(1)}, u32[]{:S(2)}, u32[]{:S(2)}) collective-permute-start(f32[3,16,4864]{2,1,0:T(8,128)} %collective-permute-done.top_ref.refs_1_), channel_id=1, source_target_pairs={{0,2},{2,4},{4,6},{6,8},{8,10},{10,12},{12,14},{14,16},{16,18},{18... | collective-permute-start | bytes 2801672 | tf_op jit(solution)/shard_map/ppermute | solution.py:24
  70.8 9.3 %copy-start.1 = (f32[3,32,4608]{2,1,0:T(8,128)}, f32[3,32,4608]{2,1,0:T(8,128)S(1)}, u32[]{:S(2)}) copy-start(f32[3,32,4608]{2,1,0:T(8,128)S(1)} %get-tuple-element.17.refs_6_) | copy-start | bytes 5308420
  70.8 20.2 %collective-permute-start.4 = (f32[3,16,4864]{2,1,0:T(8,128)S(1)}, f32[3,16,4864]{2,1,0:T(8,128)}, u32[]{:S(2)}, u32[]{:S(2)}) collective-permute-start(f32[3,16,4864]{2,1,0:T(8,128)S(1)} %collective-permute-done.1.top_ref.refs_2_), channel_id=1, source_target_pairs={{0,2},{2,4},{4,6},{6,8},{8,10},{10,12},{12,14},{14,16},{16,18},{18... | collective-permute-start | bytes 2801672 | tf_op jit(solution)/shard_map/ppermute | solution.py:24
  74.1 6.1 %copy-start.5 = (f32[3,16,4864]{2,1,0:T(8,128)}, f32[3,16,4864]{2,1,0:T(8,128)S(1)}, u32[]{:S(2)}) copy-start(f32[3,16,4864]{2,1,0:T(8,128)S(1)} %collective-permute-done.3.bottom_ref.refs_4_) | copy-start | bytes 2801668
  80.2 6.4 %copy-start.6 = (f32[3,16,4608]{2,1,0:T(8,128)}, f32[3,16,4608]{2,1,0:T(8,128)S(1)}, u32[]{:S(2)}) copy-start(f32[3,16,4608]{2,1,0:T(8,128)S(1)} %get-tuple-element.21.refs_10_) | copy-start | bytes 2654212
  80.2 8.6 %collective-permute-start.6 = (f32[3,16,4608]{2,1,0:T(8,128)S(1)}, f32[3,16,4608]{2,1,0:T(8,128)}, u32[]{:S(2)}, u32[]{:S(2)}) collective-permute-start(f32[3,16,4608]{2,1,0:T(8,128)S(1)} %get-tuple-element.21.refs_10_), channel_id=1, source_target_pairs={{2,0},{4,2},{6,4},{8,6},{10,8},{12,10},{14,12},{16,14},{18,16},{20... | collective-permute-start | bytes 2654216 | tf_op jit(solution)/shard_map/ppermute | solution.py:24
  87.5 62.4 %collective-permute-start.5 = (f32[3,32,4608]{2,1,0:T(8,128)}, f32[3,32,4608]{2,1,0:T(8,128)}, u32[]{:S(2)}, u32[]{:S(2)}) collective-permute-start(f32[3,32,4608]{2,1,0:T(8,128)} %get-tuple-element.20.refs_9_), channel_id=1, source_target_pairs={{2,0},{4,2},{6,4},{8,6},{10,8},{12,10},{14,12},{16,14},{18,16},{20... | collective-permute-start | bytes 5308424 | tf_op jit(solution)/shard_map/ppermute | solution.py:24
  91.1 7.9 %copy-start.7 = (f32[3,16,4608]{2,1,0:T(8,128)S(1)}, f32[3,16,4608]{2,1,0:T(8,128)}, u32[]{:S(2)}) copy-start(f32[3,16,4608]{2,1,0:T(8,128)} %copy-done.6) | copy-start | bytes 2654212
  97.6 54.4 %collective-permute-start.7 = (f32[3,16,4608]{2,1,0:T(8,128)}, f32[3,16,4608]{2,1,0:T(8,128)}, u32[]{:S(2)}, u32[]{:S(2)}) collective-permute-start(f32[3,16,4608]{2,1,0:T(8,128)} %get-tuple-element.22.refs_11_), channel_id=1, source_target_pairs={{2,0},{4,2},{6,4},{8,6},{10,8},{12,10},{14,12},{16,14},{18,16},{20... | collective-permute-start | bytes 2654216 | tf_op jit(solution)/shard_map/ppermute | solution.py:24
  105.7 0.6 copy-start.3
  106.3 0.6 copy-start.4
  107.0 39.2 %copy-start.10 = (f32[3,32,4608]{2,1,0:T(8,128)S(1)}, f32[3,32,4608]{2,1,0:T(8,128)}, u32[]{:S(2)}) copy-start(f32[3,32,4608]{2,1,0:T(8,128)} %pad_dynamic-slice_fusion) | copy-start | bytes 5308420
  143.1 3.1 %copy-start.17 = (f32[64,64]{1,0:T(8,128)S(1)}, f32[64,64]{1,0:T(8,128)}, u32[]{:S(2)}) copy-start(f32[64,64]{1,0:T(8,128)} %get-tuple-element.26) | copy-start | bytes 49156
  146.2 2.6 %copy-start.12 = (f32[3,16,4608]{2,1,0:T(8,128)S(1)}, f32[3,16,4608]{2,1,0:T(8,128)}, u32[]{:S(2)}) copy-start(f32[3,16,4608]{2,1,0:T(8,128)} %slice.36) | copy-start | bytes 2654212
  146.2 2.6 %copy-start.13 = (f32[3,16,4608]{2,1,0:T(8,128)S(1)}, f32[3,16,4608]{2,1,0:T(8,128)}, u32[]{:S(2)}) copy-start(f32[3,16,4608]{2,1,0:T(8,128)} %slice.31) | copy-start | bytes 2654212
  148.8 1.5 copy-start.2
  149.9 3.4 %copy-start.9 = (f32[3,16,4608]{2,1,0:T(8,128)S(1)}, f32[3,16,4608]{2,1,0:T(8,128)}, u32[]{:S(2)}) copy-start(f32[3,16,4608]{2,1,0:T(8,128)} %add.60) | copy-start | bytes 2654212
  149.9 3.4 %copy-start.15 = (f32[64,64]{1,0:T(8,128)S(1)}, f32[64,64]{1,0:T(8,128)}, u32[]{:S(2)}) copy-start(f32[64,64]{1,0:T(8,128)} %get-tuple-element.25) | copy-start | bytes 49156
  154.5 35.5 %collective-permute-start.9 = (f32[16,3,4608]{2,0,1:T(8,128)S(1)}, f32[16,3,4608]{2,0,1:T(8,128)S(1)}, u32[]{:S(2)}, u32[]{:S(2)}) collective-permute-start(f32[16,3,4608]{2,0,1:T(8,128)S(1)} %convolution_subtract_fusion.1), channel_id=1, source_target_pairs={{0,1},{1,0},{2,3},{3,2},{4,5},{5,4},{6,7},{7,6},{8,9},{9,8},{10,11... | collective-permute-start | bytes 2654216 | tf_op jit(solution)/shard_map/ppermute | solution.py:323
  156.3 32.8 %collective-permute-start.8 = (f32[16,3,4608]{2,0,1:T(8,128)S(1)}, f32[16,3,4608]{2,0,1:T(8,128)S(1)}, u32[]{:S(2)}, u32[]{:S(2)}) collective-permute-start(f32[16,3,4608]{2,0,1:T(8,128)S(1)} %convolution_subtract_fusion.2), channel_id=1, source_target_pairs={{0,1},{1,0},{2,3},{3,2},{4,5},{5,4},{6,7},{7,6},{8,9},{9,8},{10,11... | collective-permute-start | bytes 2654216 | tf_op jit(solution)/shard_map/ppermute | solution.py:323
  161.0 30.0 %copy-start.16 = (f32[64,64]{1,0:T(8,128)S(1)}, f32[64,64]{1,0:T(8,128)}, u32[]{:S(2)}) copy-start(f32[64,64]{1,0:T(8,128)} %get-tuple-element.33) | copy-start | bytes 49156
  191.0 1.8 copy-start.11

commit v4 on v3

--- a/solution.py
+++ b/solution.py
@@ -342,7 +342,7 @@
     padded = jnp.pad(vectors, ((0, 0), (0, 0), (MARGIN, MARGIN)))
     pieces = 2 if mode_count % 16 == 0 else 1
     rows = mode_count // pieces
-    tops = []
+    tops, bottoms, force_tops, force_bottoms = [], [], [], []
     for s in range(groups):
         target = lax.rem(group + s, groups)
         for piece in range(1 if s == 0 else pieces):
@@ -350,14 +350,18 @@
             window = lax.dynamic_slice(
                 padded, (0, piece * rows, target * lanes_own), (comps, size, wide)
             )
-            tops.append(window if s == 0 else rotated(window, "modes", s))
-    bottoms, force_tops, force_bottoms = [], [], []
-    for index, top in enumerate(tops):
+            if s > 0:
+                if len(tops) >= 2:
+                    window, tops[-1] = lax.optimization_barrier((window, tops[-1]))
+                window = rotated(window, "modes", s)
+            tops.append(window)
+    for index in range(len(tops)):
         if index >= 2:
-            top, force_bottoms[0] = lax.optimization_barrier((top, force_bottoms[0]))
-            tops[index] = top
-        bottoms.append(shifted(top, "mesh", 1))
-        force_top, force_bottom = layer_forces(top, bottoms[-1], modulus, inside)
+            tops[index], force_bottoms[-1] = lax.optimization_barrier(
+                (tops[index], force_bottoms[-1])
+            )
+        bottoms.append(shifted(tops[index], "mesh", 1))
+        force_top, force_bottom = layer_forces(tops[index], bottoms[-1], modulus, inside)
         force_tops.append(force_top)
         force_bottoms.append(force_bottom)
     returned = [shifted(force, "mesh", -1) for force in force_bottoms]
@@ -365,21 +369,18 @@
     ritz_matrix, rotate, mixed_rotate = ritz_solve(part_stiff, part_mass, mode_count, total_dofs)
     middle = slice(MARGIN, MARGIN + lanes_own)
     mass = jnp.concatenate([t[:, :, middle] for t in tops], 1) * density
-    image = jnp.concatenate([f + r for f, r in zip(force_tops, returned)], 1)
+    image = jnp.concatenate(force_tops, 1) + jnp.concatenate(returned, 1)
     parts = []
     for s in reversed(range(groups)):
-        for piece in range(1 if s == 0 else pieces):
-            size = mode_count if s == 0 else rows
-            start = s * mode_count + piece * rows
-            columns = slice(start, start + size)
-            part = jnp.einsum("ckn,jk->jcn", image, rotate[columns], precision=high)
-            part = part - jnp.einsum("ckn,jk->jcn", mass, mixed_rotate[columns], precision=high)
-            parts.append((s, piece * rows, part if s == 0 else rotated(part, "modes", -s)))
+        columns = slice(s * mode_count, (s + 1) * mode_count)
+        part = jnp.einsum("ckn,jk->jcn", image, rotate[columns], precision=high)
+        part = part - jnp.einsum("ckn,jk->jcn", mass, mixed_rotate[columns], precision=high)
+        parts.append(part if s == 0 else rotated(part, "modes", -s))
     parts = parts[::-1]
     residual = jnp.zeros((mode_count, comps, nodes), jnp.float32)
-    for s, start, part in parts:
+    for s, part in enumerate(parts):
         source = lax.rem(group + s, groups)
-        residual = lax.dynamic_update_slice(residual, part, (start, 0, source * lanes_own))
+        residual = lax.dynamic_update_slice(residual, part, (0, 0, source * lanes_own))
     return (residual[:, :, None], ritz_matrix)
 
 

time: 194 us -> 177 us (0.912)
  waiting for transfers between devices: 67.3 us -> 52.1 us
  other arithmetic: 5.47 us -> 0.25 us
  local copies, waits for them, and re-layouts: 24.4 us -> 26.9 us
    ppermute x4 -> x3, waiting for transfers between devices: 67.3 us -> 52 us  [rotated(): return lax.ppermute(x, axis, [(i, (i + by) % size) for i in range(size)])]
    add x3 -> x0, other arithmetic: 5.22 us -> none  [per_device(): image = jnp.concatenate([f + r for f, r in zip(force_tops, returned)], 1)]
    dot_general x3 -> x2, matrix products: 6.72 us -> 4.11 us  [per_device(): jnp.einsum('ckn,jk->jcn', mass, mixed_rotate[columns], precision=high)]
    dot_general x3 -> x2, matrix products: 3.66 us -> 5.85 us  [per_device(): part = jnp.einsum('ckn,jk->jcn', image, rotate[columns], precision=high)]
    unnamed x40 -> x46, local copies, waits for them, and re-layouts: 7.85 us -> 9.64 us
    ppermute x4 -> x3, starting transfers between devices: 4.54 us -> 5.93 us  [rotated(): return lax.ppermute(x, axis, [(i, (i + by) % size) for i in range(size)])]
    dynamic_update_slice x3 -> x2, local copies, waits for them, and re-layouts: 4.13 us -> 3.9 us  [per_device(): lax.dynamic_update_slice(residual, part, (0, 0, source * lanes_own))]
  transfers between devices with their start and end apart: 10 -> 9, of which waited for: 2 -> 4; matrix products, arithmetic and copies ran while one was open for 14% -> 11% of each run, Pallas kernels for 35% -> 39%
where the time goes in v4:
time: 177 us; the launch traced here: 176 us
  Pallas kernels  68.2 us (39%)
  waiting for transfers between devices  52.1 us (29%)
  local copies, waits for them, and re-layouts  26.9 us (15%)
  starting transfers between devices  17.5 us (10%)
  matrix products  9.96 us (6%)
    ppermute x3, waiting for transfers between devices, rotated(): return lax.ppermute(x, axis, [(i, (i + by) % size) for i in range(size)])  52 us
    pallas_call x1, Pallas kernels, ritz_solve(): pl.pallas_call(functools.partial(ritz_kernel, axes, mode_count, total_dof...  38 us
    pallas_call x3, Pallas kernels, layer_forces(): pl.pallas_call(functools.partial(layer_kernel, chunk, lanes_own), grid=(m...  23.5 us
    ppermute x6, starting transfers between devices, shifted(): return lax.ppermute(x, axis, pairs)  11.6 us
    unnamed x46, local copies, waits for them, and re-layouts  9.64 us
    pallas_call x1, Pallas kernels, grams(): pl.pallas_call(functools.partial(gram_kernel, len(tops), density.shape[1]...  6.73 us
    slice x3, local copies, waits for them, and re-layouts, per_device(): mass = jnp.concatenate([t[:, :, middle] for t in tops], 1) * density  5.99 us
    ppermute x3, starting transfers between devices, rotated(): return lax.ppermute(x, axis, [(i, (i + by) % size) for i in range(size)])  5.93 us
  transfers between devices with their start and end apart: 9, of which 4 were waited for; matrix products, arithmetic and copies ran while one was open for 11% of the time, Pallas kernels for 39%

profile of v4, /device:TPU:0, one launch (start us, length us, event | category | flops | bytes accessed | tf_op | source)
XLA Modules:
  0.0 175.9 jit_solution(13256096905309863987)
XLA Ops:
  0.6 4.4 %copy.15 = f32[32,3,1,9216]{3,0,1,2:T(8,128)} copy(f32[32,3,1,9216]{3,2,1,0:T(1,128)} %param.4) | data formatting | bytes 7077888 | tf_op args[0]
  5.0 2.5 %pad_dynamic-slice_fusion.1 = (f32[3,16,4864]{2,1,0:T(8,128)S(1)}, f32[3,16,4864]{2,1,0:T(8,128)}) fusion(s32[]{:T(128)S(6)} %select_n.32, f32[3,32,9216]{2,1,0:T(8,128)} %bitcast.21), kind=kLoop, calls=%fused_computation.7 | loop fusion | bytes 5406724 | tf_op jit(solution)/shard_map/dynamic_slice | solution.py:350
  7.6 3.0 %collective-permute-start = (f32[3,16,4864]{2,1,0:T(8,128)S(1)}, f32[3,16,4864]{2,1,0:T(8,128)S(1)}, u32[]{:S(2)}, u32[]{:S(2)}) collective-permute-start(f32[3,16,4864]{2,1,0:T(8,128)S(1)} %get-tuple-element.32), channel_id=1, source_target_pairs={{0,1},{1,0},{2,3},{3,2},{4,5},{5,4},{6,7},{7,6},{8,9},{9,8},{10,11... | collective-permute-start | bytes 2801672 | tf_op jit(solution)/shard_map/ppermute | solution.py:323
  10.5 2.9 %pad_dynamic-slice_fusion.3.top_ref.refs_0_ = f32[3,32,4864]{2,1,0:T(8,128)} fusion(s32[]{:T(128)S(6)} %select_n.31, f32[3,32,9216]{2,1,0:T(8,128)} %bitcast.21), kind=kLoop, calls=%fused_computation.9 | loop fusion | bytes 5406724 | tf_op jit(solution)/shard_map/dynamic_slice | solution.py:350
  13.4 2.7 %collective-permute-start.3 = (f32[3,32,4864]{2,1,0:T(8,128)}, f32[3,32,4864]{2,1,0:T(8,128)}, u32[]{:S(2)}, u32[]{:S(2)}) collective-permute-start(f32[3,32,4864]{2,1,0:T(8,128)} %pad_dynamic-slice_fusion.3.top_ref.refs_0_), channel_id=1, source_target_pairs={{0,2},{2,4},{4,6},{6,8},{8,10},{10,12},{12,14},{14,16},{16,18},{18... | collective-permute-start | bytes 5603336 | tf_op jit(solution)/shard_map/ppermute | solution.py:24
  16.1 0.2 select_reduce_fusion
  16.3 14.9 %collective-permute-done.top_ref.refs_1_ = f32[3,16,4864]{2,1,0:T(8,128)S(1)} collective-permute-done((f32[3,16,4864]{2,1,0:T(8,128)S(1)}, f32[3,16,4864]{2,1,0:T(8,128)S(1)}, u32[]{:S(2)}, u32[]{:S(2)}) %collective-permute-start) | collective-permute-done | bytes 933920 | tf_op jit(solution)/shard_map/ppermute | solution.py:323
  31.2 1.3 collective-permute-start.2
  32.6 0.1 fusion.5
  32.7 1.8 %collective-permute-start.1 = (f32[3,16,4864]{2,1,0:T(8,128)}, f32[3,16,4864]{2,1,0:T(8,128)}, u32[]{:S(2)}, u32[]{:S(2)}) collective-permute-start(f32[3,16,4864]{2,1,0:T(8,128)} %get-tuple-element.18), channel_id=1, source_target_pairs={{0,1},{1,0},{2,3},{3,2},{4,5},{5,4},{6,7},{7,6},{8,9},{9,8},{10,11... | collective-permute-start | bytes 2801672 | tf_op jit(solution)/shard_map/ppermute | solution.py:323
  34.5 0.2 collective-permute-done.2.bottom_ref.refs_4_
  34.6 1.0 copy-done.4
  35.6 1.2 copy-done.5
  36.8 5.5 %shard_map.62 = (f32[3,16,4608]{2,1,0:T(8,128)S(1)}, f32[3,16,4608]{2,1,0:T(8,128)}) custom-call(f32[3,16,4864]{2,1,0:T(8,128)S(1)} %collective-permute-done.top_ref.refs_1_, f32[3,16,4864]{2,1,0:T(8,128)S(1)} %copy-done.5, f32[1,4864]{1,0:T(1,128)S(1)} %pad_dynamic-slice_fusion.4.modulus_ref, f32[1,4864]{1,0:T(1,128)S(1)} %copy-done.7), custom_call_target="tpu_custom_call" | custom-call | flops 8404992000 | bytes 3735552 | tf_op jit(solution)/shard_map/pallas_call | solution.py:135
  42.3 12.8 %collective-permute-done.1.top_ref.refs_2_ = f32[3,16,4864]{2,1,0:T(8,128)} collective-permute-done((f32[3,16,4864]{2,1,0:T(8,128)}, f32[3,16,4864]{2,1,0:T(8,128)}, u32[]{:S(2)}, u32[]{:S(2)}) %collective-permute-start.1) | collective-permute-done | bytes 933920 | tf_op jit(solution)/shard_map/ppermute | solution.py:323
  55.1 3.4 %collective-permute-start.4 = (f32[3,16,4864]{2,1,0:T(8,128)}, f32[3,16,4864]{2,1,0:T(8,128)S(1)}, u32[]{:S(2)}, u32[]{:S(2)}) collective-permute-start(f32[3,16,4864]{2,1,0:T(8,128)} %collective-permute-done.1.top_ref.refs_2_), channel_id=1, source_target_pairs={{0,2},{2,4},{4,6},{6,8},{8,10},{10,12},{12,14},{14,16},{16,18},{18... | collective-permute-start | bytes 2801672 | tf_op jit(solution)/shard_map/ppermute | solution.py:24
  58.5 0.0 collective-permute-done.3.bottom_ref.refs_3_
  58.5 11.2 %shard_map.63 = (f32[3,32,4608]{2,1,0:T(8,128)S(1)}, f32[3,32,4608]{2,1,0:T(8,128)}) custom-call(f32[3,32,4864]{2,1,0:T(8,128)} %pad_dynamic-slice_fusion.3.top_ref.refs_0_, f32[3,32,4864]{2,1,0:T(8,128)} %collective-permute-done.3.bottom_ref.refs_3_, f32[1,4864]{1,0:T(1,128)S(1)} %pad_dynamic-slice_fusion.4.modulus_ref, f32[1,4864]{1,0:T(1,128)S(1)} %copy-done.7), custom_call_target="tpu_custom_call" | custom-call | flops 16809984000 | bytes 7471104 | tf_op jit(solution)/shard_map/pallas_call | solution.py:135
  69.7 1.3 collective-permute-start.5
  71.0 1.3 collective-permute-start.6
  72.3 0.0 collective-permute-done.4.bottom_ref.refs_5_
  72.4 6.7 %shard_map.64 = (f32[3,16,4608]{2,1,0:T(8,128)S(1)}, f32[3,16,4608]{2,1,0:T(8,128)}) custom-call(f32[3,16,4864]{2,1,0:T(8,128)} %collective-permute-done.1.top_ref.refs_2_, f32[3,16,4864]{2,1,0:T(8,128)S(1)} %collective-permute-done.4.bottom_ref.refs_5_, f32[1,4864]{1,0:T(1,128)S(1)} %pad_dynamic-slice_fusion.4.modulus_ref, f32[1,4864]{1,0:T(1,128)S(1)} %copy-done.8), custom_call_target="tpu_custom_call" | custom-call | flops 8404992000 | bytes 3735552 | tf_op jit(solution)/shard_map/pallas_call | solution.py:135
  79.1 1.6 collective-permute-start.7
  80.7 2.8 %pad_dynamic-slice_fusion = f32[3,32,4608]{2,1,0:T(8,128)} fusion(s32[]{:T(128)S(6)} %add.54, f32[3,32,9216]{2,1,0:T(8,128)} %bitcast.21), kind=kLoop, calls=%fused_computation.6 | loop fusion | bytes 5308420 | tf_op jit(solution)/shard_map/slice | solution.py:371
  83.6 0.1 dynamic-slice.3
  83.7 1.0 slice.24
  84.7 2.1 %slice.25 = f32[3,16,4608]{2,1,0:T(8,128)} slice(f32[3,16,4864]{2,1,0:T(8,128)} %collective-permute-done.1.top_ref.refs_2_), slice={[0:3], [0:16], [128:4736]} | slice | bytes 1769472 | tf_op jit(solution)/shard_map/slice | solution.py:371
  86.8 6.7 %shard_map.65 = (f32[64,64]{1,0:T(8,128)S(1)}, f32[64,64]{1,0:T(8,128)S(1)}) custom-call(f32[3,32,4864]{2,1,0:T(8,128)} %pad_dynamic-slice_fusion.3.top_ref.refs_0_, f32[3,16,4864]{2,1,0:T(8,128)S(1)} %collective-permute-done.top_ref.refs_1_, f32[3,16,4864]{2,1,0:T(8,128)} %collective-permute-done.1.top_ref.refs_2_, ...), custom_call_target="tpu_custom_call" | custom-call | flops 5000000000 | bytes 10000000 | tf_op jit(solution)/shard_map/pallas_call | solution.py:204
  93.6 0.0 copy-start.2
  93.6 0.6 copy-done.2
  94.2 0.6 copy-done.3
  94.8 38.0 %shard_map.66 = (f32[64,64]{1,0:T(8,128)}, f32[64,64]{1,0:T(8,128)}, f32[64,64]{1,0:T(8,128)}) custom-call(f32[64,64]{1,0:T(8,128)} %copy-done.2, f32[64,64]{1,0:T(8,128)} %copy-done.3), custom_call_target="tpu_custom_call" | custom-call | flops 10000000 | bytes 100000 | tf_op jit(solution)/shard_map/pallas_call | solution.py:305
  132.8 3.1 %fusion.1 = f32[32,3,4608]{2,0,1:T(8,128)S(1)} fusion(f32[3,16,4608]{2,1,0:T(8,128)} %slice.25, f32[3,16,4608]{2,1,0:T(8,128)} %slice.24, f32[3,32,4608]{2,1,0:T(8,128)} %pad_dynamic-slice_fusion, f32[4608]{0:T(1024)} %copy-done.13, f32[64,64]{1,0:T(8,128)} %get-tuple-element.30), kind=kOutput, calls=%fused_computation.10 | convolution fusion | flops 172523520 | bytes 5345280 | tf_op jit(solution)/shard_map/ckn,jk->jcn/dot_general | solution.py:377
  135.8 0.0 collective-permute-done.6
  135.9 0.0 collective-permute-done.5
  135.9 0.0 collective-permute-done.7
  135.9 0.0 copy-start.11
  135.9 2.9 %convolution_subtract_fusion = f32[32,3,4608]{2,0,1:T(8,128)S(1)} fusion(f32[32,3,4608]{2,0,1:T(8,128)S(1)} %fusion.1, f32[64,64]{1,0:T(8,128)S(1)} %copy-done.18, f32[3,16,4608]{2,1,0:T(8,128)S(1)} %get-tuple-element.23.refs_8_, f32[3,16,4608]{2,1,0:T(8,128)S(1)} %get-tuple-element.22.refs_7_, f32[3,32,4608]{2,1,0:T(8,128)S(1)} %copy-done.1, ...), kind=kOutput, calls=%fused_computation | convolution fusion | flops 174735360 | bytes 10633216 | tf_op jit(solution)/shard_map/ckn,jk->jcn/dot_general | solution.py:376
  138.8 1.2 collective-permute-start.8
  140.0 1.0 fusion.2
  141.1 3.0 %fusion = f32[32,3,1,4608]{3,0,1,2:T(8,128)S(1)} fusion(f32[32,3,4608]{2,0,1:T(8,128)S(1)} %fusion.2, f32[64,64]{1,0:T(8,128)S(1)} %copy-done.18, f32[3,16,4608]{2,1,0:T(8,128)S(1)} %get-tuple-element.23.refs_8_, f32[3,16,4608]{2,1,0:T(8,128)S(1)} %get-tuple-element.22.refs_7_, f32[3,32,4608]{2,1,0:T(8,128)S(1)} %copy-done.1, ...), kind=kOutput, calls=%fused_computation.2 | convolution fusion | flops 174735360 | bytes 10633216 | tf_op jit(solution)/shard_map/ckn,jk->jcn/dot_general | solution.py:376
  144.1 1.8 %broadcast_in_dim.23 = f32[32,3,1,9216]{3,2,1,0:T(1,128)S(1)} broadcast(f32[]{:T(128)} %constant.11.clone.1), dimensions={} | broadcast | bytes 3538948 | tf_op jit(solution)/shard_map/broadcast_in_dim | solution.py:384
  145.9 2.0 %copy_dynamic-update-slice_fusion.1 = f32[32,3,1,9216]{3,2,1,0:T(1,128)S(1)} fusion(f32[32,3,1,9216]{3,2,1,0:T(1,128)S(1)} %broadcast_in_dim.23, s32[]{:T(128)S(6)} %select_n.36, f32[32,3,1,4608]{3,0,1,2:T(8,128)S(1)} %fusion), kind=kLoop, calls=%fused_computation.13 | loop fusion | bytes 3538948 | tf_op jit(solution)/shard_map/dynamic_update_slice | solution.py:383
  147.9 24.3 %collective-permute-done.8 = f32[32,3,4608]{2,0,1:T(8,128)S(1)} collective-permute-done((f32[32,3,4608]{2,0,1:T(8,128)S(1)}, f32[32,3,4608]{2,0,1:T(8,128)S(1)}, u32[]{:S(2)}, u32[]{:S(2)}) %collective-permute-start.8) | collective-permute-done | bytes 1769504 | tf_op jit(solution)/shard_map/ppermute | solution.py:323
  172.1 1.9 %copy_dynamic-update-slice_fusion = f32[32,3,1,9216]{3,2,1,0:T(1,128)S(1)} fusion(f32[32,3,1,9216]{3,2,1,0:T(1,128)S(1)} %copy_dynamic-update-slice_fusion.1, s32[]{:T(128)S(6)} %select_n.37, f32[32,3,1,4608]{3,0,1,2:T(8,128)S(1)} %bitcast.22), kind=kLoop, calls=%fused_computation.12 | loop fusion | bytes 3538948 | tf_op jit(solution)/shard_map/dynamic_update_slice | solution.py:383
  174.1 0.0 copy-start.12
  174.1 0.7 copy.19
  174.8 1.1 copy-done.12
  (38 shorter events, 0.1 us)
Async XLA Ops:
  7.6 8.5 %copy-start.17 = (s32[1,9216]{1,0:T(1,128)S(1)}, s32[1,9216]{1,0:T(1,128)}, u32[]{:S(2)}) copy-start(s32[1,9216]{1,0:T(1,128)} %param.5) | copy-start | bytes 110596
  7.6 8.5 %copy-start.21 = (f32[16]{0:T(128)S(1)}, f32[16]{0:T(128)}, u32[]{:S(2)}) copy-start(f32[16]{0:T(128)} %param.6) | copy-start | bytes 196
  7.6 28.0 %copy-start.7 = (f32[1,4864]{1,0:T(1,128)S(1)}, f32[1,4864]{1,0:T(1,128)}, u32[]{:S(2)}) copy-start(f32[1,4864]{1,0:T(1,128)} %constant.33.clone.inside_ref) | copy-start | bytes 58372
  7.6 23.7 %collective-permute-start = (f32[3,16,4864]{2,1,0:T(8,128)S(1)}, f32[3,16,4864]{2,1,0:T(8,128)S(1)}, u32[]{:S(2)}, u32[]{:S(2)}) collective-permute-start(f32[3,16,4864]{2,1,0:T(8,128)S(1)} %get-tuple-element.32), channel_id=1, source_target_pairs={{0,1},{1,0},{2,3},{3,2},{4,5},{5,4},{6,7},{7,6},{8,9},{9,8},{10,11... | collective-permute-start | bytes 2801672 | tf_op jit(solution)/shard_map/ppermute | solution.py:323
  13.4 45.1 %collective-permute-start.3 = (f32[3,32,4864]{2,1,0:T(8,128)}, f32[3,32,4864]{2,1,0:T(8,128)}, u32[]{:S(2)}, u32[]{:S(2)}) collective-permute-start(f32[3,32,4864]{2,1,0:T(8,128)} %pad_dynamic-slice_fusion.3.top_ref.refs_0_), channel_id=1, source_target_pairs={{0,2},{2,4},{4,6},{6,8},{8,10},{10,12},{12,14},{14,16},{16,18},{18... | collective-permute-start | bytes 5603336 | tf_op jit(solution)/shard_map/ppermute | solution.py:24
  16.3 18.2 %copy-start.15 = (f32[9216]{0:T(1024)}, f32[9216]{0:T(1024)S(1)}, u32[]{:S(2)}) copy-start(f32[9216]{0:T(1024)S(1)} %select_reduce_fusion) | copy-start | bytes 110596
  31.2 3.4 %collective-permute-start.2 = (f32[3,16,4864]{2,1,0:T(8,128)S(1)}, f32[3,16,4864]{2,1,0:T(8,128)S(1)}, u32[]{:S(2)}, u32[]{:S(2)}) collective-permute-start(f32[3,16,4864]{2,1,0:T(8,128)S(1)} %collective-permute-done.top_ref.refs_1_), channel_id=1, source_target_pairs={{0,2},{2,4},{4,6},{6,8},{8,10},{10,12},{12,14},{14,16},{16,18},{18... | collective-permute-start | bytes 2801672 | tf_op jit(solution)/shard_map/ppermute | solution.py:24
  32.7 22.5 %collective-permute-start.1 = (f32[3,16,4864]{2,1,0:T(8,128)}, f32[3,16,4864]{2,1,0:T(8,128)}, u32[]{:S(2)}, u32[]{:S(2)}) collective-permute-start(f32[3,16,4864]{2,1,0:T(8,128)} %get-tuple-element.18), channel_id=1, source_target_pairs={{0,1},{1,0},{2,3},{3,2},{4,5},{5,4},{6,7},{7,6},{8,9},{9,8},{10,11... | collective-permute-start | bytes 2801672 | tf_op jit(solution)/shard_map/ppermute | solution.py:323
  34.6 1.0 copy-start.4
  35.6 1.2 copy-start.5
  55.1 17.2 %copy-start.8 = (f32[1,4864]{1,0:T(1,128)S(1)}, f32[1,4864]{1,0:T(1,128)}, u32[]{:S(2)}) copy-start(f32[1,4864]{1,0:T(1,128)} %constant.33.clone.inside_ref) | copy-start | bytes 58372
  55.1 17.2 %collective-permute-start.4 = (f32[3,16,4864]{2,1,0:T(8,128)}, f32[3,16,4864]{2,1,0:T(8,128)S(1)}, u32[]{:S(2)}, u32[]{:S(2)}) collective-permute-start(f32[3,16,4864]{2,1,0:T(8,128)} %collective-permute-done.1.top_ref.refs_2_), channel_id=1, source_target_pairs={{0,2},{2,4},{4,6},{6,8},{8,10},{10,12},{12,14},{14,16},{16,18},{18... | collective-permute-start | bytes 2801672 | tf_op jit(solution)/shard_map/ppermute | solution.py:24
  69.7 9.4 %copy-start = (f32[3,32,4608]{2,1,0:T(8,128)}, f32[3,32,4608]{2,1,0:T(8,128)S(1)}, u32[]{:S(2)}) copy-start(f32[3,32,4608]{2,1,0:T(8,128)S(1)} %get-tuple-element.21.refs_6_) | copy-start | bytes 5308420
  69.7 66.1 %collective-permute-start.5 = (f32[3,32,4608]{2,1,0:T(8,128)}, f32[3,32,4608]{2,1,0:T(8,128)}, u32[]{:S(2)}, u32[]{:S(2)}) collective-permute-start(f32[3,32,4608]{2,1,0:T(8,128)} %get-tuple-element.24.refs_9_), channel_id=1, source_target_pairs={{2,0},{4,2},{6,4},{8,6},{10,8},{12,10},{14,12},{16,14},{18,16},{20... | collective-permute-start | bytes 5308424 | tf_op jit(solution)/shard_map/ppermute | solution.py:24
  71.0 64.8 %collective-permute-start.6 = (f32[3,16,4608]{2,1,0:T(8,128)}, f32[3,16,4608]{2,1,0:T(8,128)}, u32[]{:S(2)}, u32[]{:S(2)}) collective-permute-start(f32[3,16,4608]{2,1,0:T(8,128)} %get-tuple-element.25.refs_10_), channel_id=1, source_target_pairs={{2,0},{4,2},{6,4},{8,6},{10,8},{12,10},{14,12},{16,14},{18,16},{20... | collective-permute-start | bytes 2654216 | tf_op jit(solution)/shard_map/ppermute | solution.py:24
  72.3 6.8 %copy-start.6 = (f32[3,16,4864]{2,1,0:T(8,128)}, f32[3,16,4864]{2,1,0:T(8,128)S(1)}, u32[]{:S(2)}) copy-start(f32[3,16,4864]{2,1,0:T(8,128)S(1)} %collective-permute-done.4.bottom_ref.refs_5_) | copy-start | bytes 2801668
  79.1 4.5 %copy-start.16 = (f32[9216]{0:T(1024)S(1)}, f32[9216]{0:T(1024)}, u32[]{:S(2)}) copy-start(f32[9216]{0:T(1024)} %copy-done.15) | copy-start | bytes 110596
  79.1 56.8 %collective-permute-start.7 = (f32[3,16,4608]{2,1,0:T(8,128)}, f32[3,16,4608]{2,1,0:T(8,128)}, u32[]{:S(2)}, u32[]{:S(2)}) collective-permute-start(f32[3,16,4608]{2,1,0:T(8,128)} %get-tuple-element.26.refs_11_), channel_id=1, source_target_pairs={{2,0},{4,2},{6,4},{8,6},{10,8},{12,10},{14,12},{16,14},{18,16},{20... | collective-permute-start | bytes 2654216 | tf_op jit(solution)/shard_map/ppermute | solution.py:24
  83.6 3.2 %copy-start.13 = (f32[4608]{0:T(1024)}, f32[4608]{0:T(1024)S(1)}, u32[]{:S(2)}) copy-start(f32[4608]{0:T(1024)S(1)} %dynamic-slice.3) | copy-start | bytes 55300
  93.6 0.6 copy-start.2
  94.2 0.6 copy-start.3
  94.8 41.1 %copy-start.1 = (f32[3,32,4608]{2,1,0:T(8,128)S(1)}, f32[3,32,4608]{2,1,0:T(8,128)}, u32[]{:S(2)}) copy-start(f32[3,32,4608]{2,1,0:T(8,128)} %copy-done) | copy-start | bytes 5308420
  132.8 3.1 %copy-start.18 = (f32[64,64]{1,0:T(8,128)S(1)}, f32[64,64]{1,0:T(8,128)}, u32[]{:S(2)}) copy-start(f32[64,64]{1,0:T(8,128)} %get-tuple-element.29) | copy-start | bytes 49156
  135.9 4.1 %copy-start.9 = (f32[3,32,4608]{2,1,0:T(8,128)S(1)}, f32[3,32,4608]{2,1,0:T(8,128)}, u32[]{:S(2)}) copy-start(f32[3,32,4608]{2,1,0:T(8,128)} %pad_dynamic-slice_fusion) | copy-start | bytes 5308420
  135.9 4.1 %copy-start.10 = (f32[3,16,4608]{2,1,0:T(8,128)S(1)}, f32[3,16,4608]{2,1,0:T(8,128)}, u32[]{:S(2)}) copy-start(f32[3,16,4608]{2,1,0:T(8,128)} %slice.24) | copy-start | bytes 2654212
  135.9 4.1 %copy-start.11 = (f32[3,16,4608]{2,1,0:T(8,128)S(1)}, f32[3,16,4608]{2,1,0:T(8,128)}, u32[]{:S(2)}) copy-start(f32[3,16,4608]{2,1,0:T(8,128)} %slice.25) | copy-start | bytes 2654212
  135.9 4.1 %copy-start.14 = (f32[4608]{0:T(1024)S(1)}, f32[4608]{0:T(1024)}, u32[]{:S(2)}) copy-start(f32[4608]{0:T(1024)} %copy-done.13) | copy-start | bytes 55300
  135.9 4.1 %copy-start.19 = (f32[64,64]{1,0:T(8,128)S(1)}, f32[64,64]{1,0:T(8,128)}, u32[]{:S(2)}) copy-start(f32[64,64]{1,0:T(8,128)} %get-tuple-element.30) | copy-start | bytes 49156
  138.8 33.3 %collective-permute-start.8 = (f32[32,3,4608]{2,0,1:T(8,128)S(1)}, f32[32,3,4608]{2,0,1:T(8,128)S(1)}, u32[]{:S(2)}, u32[]{:S(2)}) collective-permute-start(f32[32,3,4608]{2,0,1:T(8,128)S(1)} %convolution_subtract_fusion), channel_id=1, source_target_pairs={{0,1},{1,0},{2,3},{3,2},{4,5},{5,4},{6,7},{7,6},{8,9},{9,8},{10,11... | collective-permute-start | bytes 5308424 | tf_op jit(solution)/shard_map/ppermute | solution.py:323
  145.9 28.2 %copy-start.20 = (f32[64,64]{1,0:T(8,128)S(1)}, f32[64,64]{1,0:T(8,128)}, u32[]{:S(2)}) copy-start(f32[64,64]{1,0:T(8,128)} %get-tuple-element.37) | copy-start | bytes 49156
  174.1 1.8 %copy-start.12 = (f32[32,3,1,9216]{3,2,1,0:T(1,128)}, f32[32,3,1,9216]{3,2,1,0:T(1,128)S(1)}, u32[]{:S(2)}) copy-start(f32[32,3,1,9216]{3,2,1,0:T(1,128)S(1)} %copy_dynamic-update-slice_fusion) | copy-start | bytes 10616836

commit v5 on v4

--- a/solution.py
+++ b/solution.py
@@ -342,6 +342,7 @@
     padded = jnp.pad(vectors, ((0, 0), (0, 0), (MARGIN, MARGIN)))
     pieces = 2 if mode_count % 16 == 0 else 1
     rows = mode_count // pieces
+    middle = slice(MARGIN, MARGIN + lanes_own)
     tops, bottoms, force_tops, force_bottoms = [], [], [], []
     for s in range(groups):
         target = lax.rem(group + s, groups)
@@ -357,18 +358,19 @@
             tops.append(window)
     for index in range(len(tops)):
         if index >= 2:
-            tops[index], force_bottoms[-1] = lax.optimization_barrier(
-                (tops[index], force_bottoms[-1])
+            tops[index], force_bottoms[-1], force_bottoms[0] = lax.optimization_barrier(
+                (tops[index], force_bottoms[-1], force_bottoms[0])
             )
         bottoms.append(shifted(tops[index], "mesh", 1))
+        if index == len(tops) - 1:
+            mass = jnp.concatenate([t[:, :, middle] for t in tops], 1) * density
+            mass, bottoms[-1] = lax.optimization_barrier((mass, bottoms[-1]))
         force_top, force_bottom = layer_forces(tops[index], bottoms[-1], modulus, inside)
         force_tops.append(force_top)
         force_bottoms.append(force_bottom)
     returned = [shifted(force, "mesh", -1) for force in force_bottoms]
     part_stiff, part_mass = grams(tops, bottoms, force_tops, force_bottoms, density)
     ritz_matrix, rotate, mixed_rotate = ritz_solve(part_stiff, part_mass, mode_count, total_dofs)
-    middle = slice(MARGIN, MARGIN + lanes_own)
-    mass = jnp.concatenate([t[:, :, middle] for t in tops], 1) * density
     image = jnp.concatenate(force_tops, 1) + jnp.concatenate(returned, 1)
     parts = []
     for s in reversed(range(groups)):

time: 177 us -> 204 us (1.15)
  Pallas kernels: 68.2 us -> 99.8 us
  local copies, waits for them, and re-layouts: 26.9 us -> 22.6 us
  other arithmetic: 0.25 us -> 2.48 us
    pallas_call x1, Pallas kernels: 38 us -> 70.5 us  [ritz_solve(): pl.pallas_call(functools.partial(ritz_kernel, axes, mode_count, total_dof...]
    slice x3, local copies, waits for them, and re-layouts: 5.99 us -> 1.82 us  [per_device(): mass = jnp.concatenate([t[:, :, middle] for t in tops], 1) * density]
    mul x0 -> x1, other arithmetic: none -> 2.23 us  [per_device(): mass = jnp.concatenate([t[:, :, middle] for t in tops], 1) * density]
    unnamed x46 -> x44, local copies, waits for them, and re-layouts: 9.64 us -> 10.5 us
  transfers between devices with their start and end apart: 9 -> 9, of which waited for: 4 -> 3; matrix products, arithmetic and copies ran while one was open for 11% -> 9% of each run, Pallas kernels for 39% -> 49%
where the time goes in v5:
time: 204 us; the launch traced here: 203 us
  Pallas kernels  99.8 us (49%)
  waiting for transfers between devices  51.4 us (25%)
  local copies, waits for them, and re-layouts  22.6 us (11%)
  starting transfers between devices  15.9 us (8%)
  matrix products  10.1 us (5%)
  other arithmetic  2.48 us (1%)
    pallas_call x1, Pallas kernels, ritz_solve(): pl.pallas_call(functools.partial(ritz_kernel, axes, mode_count, total_dof...  70.5 us
    ppermute x3, waiting for transfers between devices, rotated(): return lax.ppermute(x, axis, [(i, (i + by) % size) for i in range(size)])  51.4 us
    pallas_call x3, Pallas kernels, layer_forces(): pl.pallas_call(functools.partial(layer_kernel, chunk, lanes_own), grid=(m...  22.8 us
    ppermute x6, starting transfers between devices, shifted(): return lax.ppermute(x, axis, pairs)  11.4 us
    unnamed x44, local copies, waits for them, and re-layouts  10.5 us
    pallas_call x1, Pallas kernels, grams(): pl.pallas_call(functools.partial(gram_kernel, len(tops), density.shape[1]...  6.53 us
    dot_general x2, matrix products, per_device(): part = jnp.einsum('ckn,jk->jcn', image, rotate[columns], precision=high)  5.85 us
    dynamic_slice x2, local copies, waits for them, and re-layouts, per_device(): lax.dynamic_slice(padded, (0, piece * rows, target * lanes_own), (comps,...  4.47 us
  transfers between devices with their start and end apart: 9, of which 3 were waited for; matrix products, arithmetic and copies ran while one was open for 9% of the time, Pallas kernels for 49%

profile of v5, /device:TPU:0, one launch (start us, length us, event | category | flops | bytes accessed | tf_op | source)
XLA Modules:
  0.0 203.3 jit_solution(8088818175053663393)
XLA Ops:
  0.6 4.4 %copy.15 = f32[32,3,1,9216]{3,0,1,2:T(8,128)} copy(f32[32,3,1,9216]{3,2,1,0:T(1,128)} %param.4) | data formatting | bytes 7077888 | tf_op args[0]
  5.0 1.6 pad_dynamic-slice_fusion.3.top_ref.refs_0_
  6.7 0.0 copy-start.16
  6.7 0.0 copy-start.20
  6.7 3.7 %collective-permute-start.3 = (f32[3,32,4864]{2,1,0:T(8,128)S(1)}, f32[3,32,4864]{2,1,0:T(8,128)}, u32[]{:S(2)}, u32[]{:S(2)}) collective-permute-start(f32[3,32,4864]{2,1,0:T(8,128)S(1)} %pad_dynamic-slice_fusion.3.top_ref.refs_0_), channel_id=1, source_target_pairs={{0,2},{2,4},{4,6},{6,8},{8,10},{10,12},{12,14},{14,16},{16,18},{18... | collective-permute-start | bytes 5603336 | tf_op jit(solution)/shard_map/ppermute | solution.py:24
  10.4 2.9 %pad_dynamic-slice_fusion.1 = (f32[3,16,4864]{2,1,0:T(8,128)}, f32[3,16,4864]{2,1,0:T(8,128)}) fusion(s32[]{:T(128)S(6)} %select_n.32, f32[3,32,9216]{2,1,0:T(8,128)} %bitcast.25), kind=kLoop, calls=%fused_computation.7 | loop fusion | bytes 5406724 | tf_op jit(solution)/shard_map/dynamic_slice | solution.py:351
  13.3 2.4 %collective-permute-start = (f32[3,16,4864]{2,1,0:T(8,128)}, f32[3,16,4864]{2,1,0:T(8,128)S(1)}, u32[]{:S(2)}, u32[]{:S(2)}) collective-permute-start(f32[3,16,4864]{2,1,0:T(8,128)} %get-tuple-element.38), channel_id=1, source_target_pairs={{0,1},{1,0},{2,3},{3,2},{4,5},{5,4},{6,7},{7,6},{8,9},{9,8},{10,11... | collective-permute-start | bytes 2801672 | tf_op jit(solution)/shard_map/ppermute | solution.py:323
  15.6 0.2 select_reduce_fusion
  15.8 0.1 fusion.1
  15.9 0.1 dynamic-slice.3
  16.0 0.0 copy-start.12
  16.0 1.7 pad_dynamic-slice_fusion
  17.7 19.6 %collective-permute-done.top_ref.refs_1_ = f32[3,16,4864]{2,1,0:T(8,128)S(1)} collective-permute-done((f32[3,16,4864]{2,1,0:T(8,128)}, f32[3,16,4864]{2,1,0:T(8,128)S(1)}, u32[]{:S(2)}, u32[]{:S(2)}) %collective-permute-start) | collective-permute-done | bytes 933920 | tf_op jit(solution)/shard_map/ppermute | solution.py:323
  37.3 2.1 %collective-permute-start.2 = (f32[3,16,4864]{2,1,0:T(8,128)S(1)}, f32[3,16,4864]{2,1,0:T(8,128)S(1)}, u32[]{:S(2)}, u32[]{:S(2)}) collective-permute-start(f32[3,16,4864]{2,1,0:T(8,128)S(1)} %collective-permute-done.top_ref.refs_1_), channel_id=1, source_target_pairs={{0,2},{2,4},{4,6},{6,8},{8,10},{10,12},{12,14},{14,16},{16,18},{18... | collective-permute-start | bytes 2801672 | tf_op jit(solution)/shard_map/ppermute | solution.py:24
  39.4 0.1 slice.22
  39.4 1.5 collective-permute-start.1
  41.0 11.4 %shard_map.63 = (f32[3,32,4608]{2,1,0:T(8,128)S(1)}, f32[3,32,4608]{2,1,0:T(8,128)}) custom-call(f32[3,32,4864]{2,1,0:T(8,128)S(1)} %pad_dynamic-slice_fusion.3.top_ref.refs_0_, f32[3,32,4864]{2,1,0:T(8,128)} %collective-permute-done.3.bottom_ref.refs_3_, f32[1,4864]{1,0:T(1,128)S(1)} %pad_dynamic-slice_fusion.4.modulus_ref, f32[1,4864]{1,0:T(1,128)S(1)} %copy-done.12), custom_call_target="tpu_custom_call" | custom-call | flops 16809984000 | bytes 7471104 | tf_op jit(solution)/shard_map/pallas_call | solution.py:135
  52.4 0.0 collective-permute-done.2.bottom_ref.refs_4_
  52.4 1.8 copy-done.4
  54.2 5.7 %shard_map.62 = (f32[3,16,4608]{2,1,0:T(8,128)S(1)}, f32[3,16,4608]{2,1,0:T(8,128)}) custom-call(f32[3,16,4864]{2,1,0:T(8,128)S(1)} %copy-done.4, f32[3,16,4864]{2,1,0:T(8,128)S(1)} %collective-permute-done.2.bottom_ref.refs_4_, f32[1,4864]{1,0:T(1,128)S(1)} %pad_dynamic-slice_fusion.4.modulus_ref, f32[1,4864]{1,0:T(1,128)S(1)} %copy-done.12), custom_call_target="tpu_custom_call" | custom-call | flops 8404992000 | bytes 3735552 | tf_op jit(solution)/shard_map/pallas_call | solution.py:135
  59.9 2.6 %collective-permute-done.1.top_ref.refs_2_ = f32[3,16,4864]{2,1,0:T(8,128)S(1)} collective-permute-done((f32[3,16,4864]{2,1,0:T(8,128)S(1)}, f32[3,16,4864]{2,1,0:T(8,128)S(1)}, u32[]{:S(2)}, u32[]{:S(2)}) %collective-permute-start.1) | collective-permute-done | bytes 933920 | tf_op jit(solution)/shard_map/ppermute | solution.py:323
  62.5 0.1 slice.23
  62.6 1.6 collective-permute-start.4
  64.2 1.3 collective-permute-start.5
  65.5 1.3 collective-permute-start.6
  66.8 2.2 %maximum_multiply_fusion = f32[3,64,4608]{2,1,0:T(8,128)} fusion(f32[3,16,4608]{2,1,0:T(8,128)S(1)} %slice.23, f32[3,16,4608]{2,1,0:T(8,128)S(1)} %slice.22, f32[3,32,4608]{2,1,0:T(8,128)S(1)} %pad_dynamic-slice_fusion, f32[4608]{0:T(1024)S(1)} %dynamic-slice.3), kind=kLoop, calls=%fused_computation.3 | loop fusion | flops 2654208 | bytes 7096320 | tf_op jit(solution)/shard_map/mul | solution.py:366
  69.0 0.0 collective-permute-done.4.bottom_ref.refs_5_
  69.1 5.7 %shard_map.64 = (f32[3,16,4608]{2,1,0:T(8,128)S(1)}, f32[3,16,4608]{2,1,0:T(8,128)}) custom-call(f32[3,16,4864]{2,1,0:T(8,128)S(1)} %collective-permute-done.1.top_ref.refs_2_, f32[3,16,4864]{2,1,0:T(8,128)S(1)} %collective-permute-done.4.bottom_ref.refs_5_, f32[1,4864]{1,0:T(1,128)S(1)} %pad_dynamic-slice_fusion.4.modulus_ref, f32[1,4864]{1,0:T(1,128)S(1)} %copy-done.12), custom_call_target="tpu_custom_call" | custom-call | flops 8404992000 | bytes 3735552 | tf_op jit(solution)/shard_map/pallas_call | solution.py:135
  74.7 1.5 collective-permute-start.7
  76.3 1.2 copy-done.7
  77.4 6.5 %shard_map.65 = (f32[64,64]{1,0:T(8,128)S(1)}, f32[64,64]{1,0:T(8,128)S(1)}) custom-call(f32[3,32,4864]{2,1,0:T(8,128)} %copy-done.2, f32[3,16,4864]{2,1,0:T(8,128)S(1)} %copy-done.5, f32[3,16,4864]{2,1,0:T(8,128)S(1)} %copy-done.7, f32[3,32,4864]{2,1,0:T(8,128)} %collective-permute-done.3.bottom_ref.refs_3_, f32[3,16,4864]{2,1,0:T(8,128)} %copy-done.10, ...), custom_call_target="tpu_custom_call" | custom-call | flops 5000000000 | bytes 10000000 | tf_op jit(solution)/shard_map/pallas_call | solution.py:204
  84.0 0.0 copy-start.8
  84.0 0.6 copy-done.8
  84.6 0.6 copy-done.9
  85.2 70.5 %shard_map.66 = (f32[64,64]{1,0:T(8,128)}, f32[64,64]{1,0:T(8,128)}, f32[64,64]{1,0:T(8,128)}) custom-call(f32[64,64]{1,0:T(8,128)} %copy-done.8, f32[64,64]{1,0:T(8,128)} %copy-done.9), custom_call_target="tpu_custom_call" | custom-call | flops 10000000 | bytes 100000 | tf_op jit(solution)/shard_map/pallas_call | solution.py:305
  155.7 3.1 %fusion.2 = f32[32,3,4608]{2,0,1:T(8,128)S(1)} fusion(f32[3,64,4608]{2,1,0:T(8,128)} %maximum_multiply_fusion, f32[64,64]{1,0:T(8,128)} %get-tuple-element.35), kind=kOutput, calls=%fused_computation.17 | convolution fusion | flops 169869312 | bytes 5324800 | tf_op jit(solution)/shard_map/ckn,jk->jcn/dot_general | solution.py:379
  158.8 0.0 copy-start.13
  158.9 2.9 %convolution_subtract_fusion = f32[32,3,4608]{2,0,1:T(8,128)S(1)} fusion(f32[32,3,4608]{2,0,1:T(8,128)S(1)} %fusion.2, f32[64,64]{1,0:T(8,128)S(1)} %copy-done.17, f32[3,16,4608]{2,1,0:T(8,128)S(1)} %get-tuple-element.28.refs_8_, f32[3,16,4608]{2,1,0:T(8,128)S(1)} %get-tuple-element.27.refs_7_, f32[3,32,4608]{2,1,0:T(8,128)S(1)} %copy-done.1, ...), kind=kOutput, calls=%fused_computation | convolution fusion | flops 174735360 | bytes 10633216 | tf_op jit(solution)/shard_map/ckn,jk->jcn/dot_general | solution.py:378
  161.8 0.6 collective-permute-start.8
  162.3 1.2 fusion.5
  163.5 3.0 %fusion = f32[32,3,1,4608]{3,0,1,2:T(8,128)S(1)} fusion(f32[32,3,4608]{2,0,1:T(8,128)S(1)} %fusion.5, f32[64,64]{1,0:T(8,128)S(1)} %copy-done.17, f32[3,16,4608]{2,1,0:T(8,128)S(1)} %get-tuple-element.28.refs_8_, f32[3,16,4608]{2,1,0:T(8,128)S(1)} %get-tuple-element.27.refs_7_, f32[3,32,4608]{2,1,0:T(8,128)S(1)} %copy-done.1, ...), kind=kOutput, calls=%fused_computation.2 | convolution fusion | flops 174735360 | bytes 10633216 | tf_op jit(solution)/shard_map/ckn,jk->jcn/dot_general | solution.py:378
  166.5 1.8 broadcast_in_dim.23
  168.3 2.0 copy_dynamic-update-slice_fusion.1
  170.3 29.2 %collective-permute-done.8 = f32[32,3,4608]{2,0,1:T(8,128)S(1)} collective-permute-done((f32[32,3,4608]{2,0,1:T(8,128)S(1)}, f32[32,3,4608]{2,0,1:T(8,128)S(1)}, u32[]{:S(2)}, u32[]{:S(2)}) %collective-permute-start.8) | collective-permute-done | bytes 1769504 | tf_op jit(solution)/shard_map/ppermute | solution.py:323
  199.5 1.9 copy_dynamic-update-slice_fusion
  201.4 0.0 copy-start.14
  201.5 0.6 copy.19
  202.1 1.1 copy-done.14
  (37 shorter events, 0.1 us)
Async XLA Ops:
  6.7 34.3 %copy-start.2 = (f32[3,32,4864]{2,1,0:T(8,128)}, f32[3,32,4864]{2,1,0:T(8,128)S(1)}, u32[]{:S(2)}) copy-start(f32[3,32,4864]{2,1,0:T(8,128)S(1)} %pad_dynamic-slice_fusion.3.top_ref.refs_0_) | copy-start | bytes 5603332
  6.7 9.0 %copy-start.16 = (s32[1,9216]{1,0:T(1,128)S(1)}, s32[1,9216]{1,0:T(1,128)}, u32[]{:S(2)}) copy-start(s32[1,9216]{1,0:T(1,128)} %param.5) | copy-start | bytes 110596
  6.7 8.9 %copy-start.20 = (f32[16]{0:T(128)S(1)}, f32[16]{0:T(128)}, u32[]{:S(2)}) copy-start(f32[16]{0:T(128)} %param.6) | copy-start | bytes 196
  6.7 34.2 %collective-permute-start.3 = (f32[3,32,4864]{2,1,0:T(8,128)S(1)}, f32[3,32,4864]{2,1,0:T(8,128)}, u32[]{:S(2)}, u32[]{:S(2)}) collective-permute-start(f32[3,32,4864]{2,1,0:T(8,128)S(1)} %pad_dynamic-slice_fusion.3.top_ref.refs_0_), channel_id=1, source_target_pairs={{0,2},{2,4},{4,6},{6,8},{8,10},{10,12},{12,14},{14,16},{16,18},{18... | collective-permute-start | bytes 5603336 | tf_op jit(solution)/shard_map/ppermute | solution.py:24
  13.3 24.0 %collective-permute-start = (f32[3,16,4864]{2,1,0:T(8,128)}, f32[3,16,4864]{2,1,0:T(8,128)S(1)}, u32[]{:S(2)}, u32[]{:S(2)}) collective-permute-start(f32[3,16,4864]{2,1,0:T(8,128)} %get-tuple-element.38), channel_id=1, source_target_pairs={{0,1},{1,0},{2,3},{3,2},{4,5},{5,4},{6,7},{7,6},{8,9},{9,8},{10,11... | collective-permute-start | bytes 2801672 | tf_op jit(solution)/shard_map/ppermute | solution.py:323
  16.0 23.4 %copy-start.15 = (f32[3,16,4864]{2,1,0:T(8,128)S(1)}, f32[3,16,4864]{2,1,0:T(8,128)}, u32[]{:S(2)}) copy-start(f32[3,16,4864]{2,1,0:T(8,128)} %get-tuple-element.21) | copy-start | bytes 2801668
  16.0 24.9 %copy-start.12 = (f32[1,4864]{1,0:T(1,128)S(1)}, f32[1,4864]{1,0:T(1,128)}, u32[]{:S(2)}) copy-start(f32[1,4864]{1,0:T(1,128)} %constant.33.clone.inside_ref) | copy-start | bytes 58372
  37.3 15.1 %copy-start.3 = (f32[3,16,4864]{2,1,0:T(8,128)}, f32[3,16,4864]{2,1,0:T(8,128)S(1)}, u32[]{:S(2)}) copy-start(f32[3,16,4864]{2,1,0:T(8,128)S(1)} %collective-permute-done.top_ref.refs_1_) | copy-start | bytes 2801668
  37.3 15.1 %collective-permute-start.2 = (f32[3,16,4864]{2,1,0:T(8,128)S(1)}, f32[3,16,4864]{2,1,0:T(8,128)S(1)}, u32[]{:S(2)}, u32[]{:S(2)}) collective-permute-start(f32[3,16,4864]{2,1,0:T(8,128)S(1)} %collective-permute-done.top_ref.refs_1_), channel_id=1, source_target_pairs={{0,2},{2,4},{4,6},{6,8},{8,10},{10,12},{12,14},{14,16},{16,18},{18... | collective-permute-start | bytes 2801672 | tf_op jit(solution)/shard_map/ppermute | solution.py:24
  39.4 23.1 %collective-permute-start.1 = (f32[3,16,4864]{2,1,0:T(8,128)S(1)}, f32[3,16,4864]{2,1,0:T(8,128)S(1)}, u32[]{:S(2)}, u32[]{:S(2)}) collective-permute-start(f32[3,16,4864]{2,1,0:T(8,128)S(1)} %copy-done.15), channel_id=1, source_target_pairs={{0,1},{1,0},{2,3},{3,2},{4,5},{5,4},{6,7},{7,6},{8,9},{9,8},{10,11... | collective-permute-start | bytes 2801672 | tf_op jit(solution)/shard_map/ppermute | solution.py:323
  52.4 7.5 %copy-start = (f32[3,32,4608]{2,1,0:T(8,128)}, f32[3,32,4608]{2,1,0:T(8,128)S(1)}, u32[]{:S(2)}) copy-start(f32[3,32,4608]{2,1,0:T(8,128)S(1)} %get-tuple-element.26.refs_6_) | copy-start | bytes 5308420
  52.4 1.8 copy-start.4
  54.2 5.7 %copy-start.10 = (f32[3,16,4864]{2,1,0:T(8,128)}, f32[3,16,4864]{2,1,0:T(8,128)S(1)}, u32[]{:S(2)}) copy-start(f32[3,16,4864]{2,1,0:T(8,128)S(1)} %collective-permute-done.2.bottom_ref.refs_4_) | copy-start | bytes 2801668
  62.5 6.5 %copy-start.6 = (f32[3,16,4864]{2,1,0:T(8,128)}, f32[3,16,4864]{2,1,0:T(8,128)S(1)}, u32[]{:S(2)}) copy-start(f32[3,16,4864]{2,1,0:T(8,128)S(1)} %collective-permute-done.1.top_ref.refs_2_) | copy-start | bytes 2801668
  62.6 6.4 %collective-permute-start.4 = (f32[3,16,4864]{2,1,0:T(8,128)S(1)}, f32[3,16,4864]{2,1,0:T(8,128)S(1)}, u32[]{:S(2)}, u32[]{:S(2)}) collective-permute-start(f32[3,16,4864]{2,1,0:T(8,128)S(1)} %collective-permute-done.1.top_ref.refs_2_), channel_id=1, source_target_pairs={{0,2},{2,4},{4,6},{6,8},{8,10},{10,12},{12,14},{14,16},{16,18},{18... | collective-permute-start | bytes 2801672 | tf_op jit(solution)/shard_map/ppermute | solution.py:24
  64.2 94.6 %collective-permute-start.5 = (f32[3,32,4608]{2,1,0:T(8,128)}, f32[3,32,4608]{2,1,0:T(8,128)}, u32[]{:S(2)}, u32[]{:S(2)}) collective-permute-start(f32[3,32,4608]{2,1,0:T(8,128)} %get-tuple-element.29.refs_9_), channel_id=1, source_target_pairs={{2,0},{4,2},{6,4},{8,6},{10,8},{12,10},{14,12},{16,14},{18,16},{20... | collective-permute-start | bytes 5308424 | tf_op jit(solution)/shard_map/ppermute | solution.py:24
  65.5 93.3 %collective-permute-start.6 = (f32[3,16,4608]{2,1,0:T(8,128)}, f32[3,16,4608]{2,1,0:T(8,128)}, u32[]{:S(2)}, u32[]{:S(2)}) collective-permute-start(f32[3,16,4608]{2,1,0:T(8,128)} %get-tuple-element.30.refs_10_), channel_id=1, source_target_pairs={{2,0},{4,2},{6,4},{8,6},{10,8},{12,10},{14,12},{16,14},{18,16},{20... | collective-permute-start | bytes 2654216 | tf_op jit(solution)/shard_map/ppermute | solution.py:24
  69.0 7.2 %copy-start.5 = (f32[3,16,4864]{2,1,0:T(8,128)S(1)}, f32[3,16,4864]{2,1,0:T(8,128)}, u32[]{:S(2)}) copy-start(f32[3,16,4864]{2,1,0:T(8,128)} %copy-done.3) | copy-start | bytes 2801668
  69.0 5.7 %copy-start.11 = (f32[3,16,4864]{2,1,0:T(8,128)}, f32[3,16,4864]{2,1,0:T(8,128)S(1)}, u32[]{:S(2)}) copy-start(f32[3,16,4864]{2,1,0:T(8,128)S(1)} %collective-permute-done.4.bottom_ref.refs_5_) | copy-start | bytes 2801668
  74.7 84.1 %collective-permute-start.7 = (f32[3,16,4608]{2,1,0:T(8,128)}, f32[3,16,4608]{2,1,0:T(8,128)}, u32[]{:S(2)}, u32[]{:S(2)}) collective-permute-start(f32[3,16,4608]{2,1,0:T(8,128)} %get-tuple-element.31.refs_11_), channel_id=1, source_target_pairs={{2,0},{4,2},{6,4},{8,6},{10,8},{12,10},{14,12},{16,14},{18,16},{20... | collective-permute-start | bytes 2654216 | tf_op jit(solution)/shard_map/ppermute | solution.py:24
  76.3 1.2 copy-start.7
  84.0 0.6 copy-start.8
  84.6 0.6 copy-start.9
  85.2 73.6 %copy-start.1 = (f32[3,32,4608]{2,1,0:T(8,128)S(1)}, f32[3,32,4608]{2,1,0:T(8,128)}, u32[]{:S(2)}) copy-start(f32[3,32,4608]{2,1,0:T(8,128)} %copy-done) | copy-start | bytes 5308420
  155.7 3.1 %copy-start.17 = (f32[64,64]{1,0:T(8,128)S(1)}, f32[64,64]{1,0:T(8,128)}, u32[]{:S(2)}) copy-start(f32[64,64]{1,0:T(8,128)} %get-tuple-element.34) | copy-start | bytes 49156
  158.8 3.5 %copy-start.13 = (f32[3,64,4608]{2,1,0:T(8,128)S(1)}, f32[3,64,4608]{2,1,0:T(8,128)}, u32[]{:S(2)}) copy-start(f32[3,64,4608]{2,1,0:T(8,128)} %maximum_multiply_fusion) | copy-start | bytes 10616836
  158.8 3.5 %copy-start.18 = (f32[64,64]{1,0:T(8,128)S(1)}, f32[64,64]{1,0:T(8,128)}, u32[]{:S(2)}) copy-start(f32[64,64]{1,0:T(8,128)} %get-tuple-element.35) | copy-start | bytes 49156
  161.8 37.7 %collective-permute-start.8 = (f32[32,3,4608]{2,0,1:T(8,128)S(1)}, f32[32,3,4608]{2,0,1:T(8,128)S(1)}, u32[]{:S(2)}, u32[]{:S(2)}) collective-permute-start(f32[32,3,4608]{2,0,1:T(8,128)S(1)} %convolution_subtract_fusion), channel_id=1, source_target_pairs={{0,1},{1,0},{2,3},{3,2},{4,5},{5,4},{6,7},{7,6},{8,9},{9,8},{10,11... | collective-permute-start | bytes 5308424 | tf_op jit(solution)/shard_map/ppermute | solution.py:323
  168.3 33.1 %copy-start.19 = (f32[64,64]{1,0:T(8,128)S(1)}, f32[64,64]{1,0:T(8,128)}, u32[]{:S(2)}) copy-start(f32[64,64]{1,0:T(8,128)} %get-tuple-element.43) | copy-start | bytes 49156
  201.4 1.8 copy-start.14
